TPU v7x, 128 devices: a whole 4x4x4 slice. The times are simulated.
128 devices in a mesh: section: 2 (over core), dp: 16 (over z, y), tensor: 4 (over x).
Axes of the slice: x: 4, y: 4, z: 4, core: 2. Of those that a mesh axis runs over, the one named last changes fastest.
Arguments:
- tokens: bfloat16 [32, 384, 1088], P('dp', 'tensor'), may hold values from -6 to 6
- cotangent: bfloat16 [32, 384, 1088], P('dp', 'tensor'), may hold values from -6 to 6
- doc_lengths: int32 [32, 4], P('dp'), may hold values from 1 to 336, 384 in all within a row
- norm_gains: bfloat16 [2, 2, 1088], P('section', None, 'tensor'), may hold values from 0.5 to 1.5
- w_qkv: bfloat16 [2, 1088, 3264], P('section', 'tensor'), may hold values from -0.1875 to 0.1875
- w_out: bfloat16 [2, 1088, 1088], P('section', 'tensor'), may hold values from -0.75 to 0.75
- w_up: bfloat16 [2, 1088, 4352], P('section', None, 'tensor'), may hold values from -0.1875 to 0.1875
- w_down: bfloat16 [2, 4352, 1088], P('section', 'tensor'), may hold values from -0.09375 to 0.09375
Outputs:
- activations: bfloat16 [2, 32, 384, 1088], P('section', 'dp', 'tensor')
- input_grads: bfloat16 [2, 32, 384, 1088], P('section', 'dp', 'tensor')
- grad_gains: float32 [2, 2, 1088], P('section', None, 'tensor')
- grad_qkv: float32 [2, 1088, 3264], P('section', 'tensor')
- grad_out: float32 [2, 1088, 1088], P('section', 'tensor')
- grad_up: float32 [2, 1088, 4352], P('section', None, 'tensor')
- grad_down: float32 [2, 4352, 1088], P('section', 'tensor')
Inputs may be any that keep to these rules, and one draw needn't show every extreme that they name: `doc_lengths`: each row holds the lengths of the 4 documents of one sequence, summing to 384; the longest has exactly 336 tokens.
All inputs are finite; a program needn't handle non-finite values.
Results may differ from a plain program's by a relative error of at most 0.035.
Values may be sent and summed in bfloat16 or wider, within the bound.
A program may use at most 192 MiB of HBM per device.

v0:
```python
import jax
import jax.numpy as jnp
from jax import lax
from jax.sharding import PartitionSpec as P

HEAD_DIM = 64


def passed_along(block, axis, distance):
    devices = range(lax.axis_size(axis))
    route = [(i - distance, i) for i in devices if i - distance in devices]
    return lax.ppermute(block, axis, route)


def norm_rows(values, norm_gain):
    average = jnp.mean(values, axis=-1, keepdims=True)
    centered = values - average
    variance = jnp.mean(centered * centered, axis=-1, keepdims=True)
    return centered * lax.rsqrt(variance + 1e-05) * norm_gain


def gelu_tanh(values):
    inner = 0.7978845608028654 * (values + 0.044715 * values * values * values)
    return 0.5 * values * (1.0 + jnp.tanh(inner))


def doc_numbers(lengths, places):
    doc_ends = jnp.cumsum(lengths)
    return jnp.sum((places[:, None] >= doc_ends[None, :]).astype(jnp.int32), axis=1)


def contract_last(left, right):
    return lax.dot_general(
        left, right, (((1,), (1,)), ((), ())), preferred_element_type=jnp.float32
    )


def contract_first(left, right):
    return lax.dot_general(
        left, right, (((0,), (0,)), ((), ())), preferred_element_type=jnp.float32
    )


def attend(query_heads, key_heads, allowed):
    scores = jnp.einsum(
        "qhd,khd->hqk", query_heads, key_heads, preferred_element_type=jnp.float32
    ) * HEAD_DIM ** (-0.5)
    scores = jnp.where(allowed[None], scores, -1e30)
    row_max = jnp.max(scores, axis=-1, keepdims=True)
    raised = jnp.exp(scores - row_max)
    return raised / jnp.sum(raised, axis=-1, keepdims=True)


def body(tokens, cotangent, doc_lengths, norm_gains, w_qkv, w_out, w_up, w_down):
    batches, rows_own, features = tokens.shape
    tensor_size = lax.axis_size("tensor")
    seq_rows = rows_own * tensor_size
    head_count = features // HEAD_DIM
    is_first = lax.axis_index("section") == 0
    qkv_full, out_full, gains_low = (
        lax.all_gather(w_qkv[0], "tensor", axis=0, tiled=True),
        lax.all_gather(w_out[0], "tensor", axis=0, tiled=True),
        lax.all_gather(norm_gains[0], "tensor", axis=1, tiled=True),
    )
    gains_full = gains_low.astype(jnp.float32)
    up_local = w_up[0]
    down_local = w_down[0]
    own_places = lax.axis_index("tensor") * rows_own + jnp.arange(rows_own, dtype=jnp.int32)
    all_places = jnp.arange(seq_rows, dtype=jnp.int32)
    masks = []
    for which in range(batches):
        own_docs = doc_numbers(doc_lengths[which], own_places)
        all_docs = doc_numbers(doc_lengths[which], all_places)
        masks.append(
            (all_places[None, :] <= own_places[:, None]) & (all_docs[None, :] == own_docs[:, None])
        )

    def split_heads(block):
        return block.reshape(block.shape[0], head_count, HEAD_DIM)

    def forward_layer(inputs, allowed):
        normed_one = norm_rows(inputs, gains_full[0]).astype(jnp.bfloat16)
        projected = jnp.dot(normed_one, qkv_full, preferred_element_type=jnp.float32).astype(
            jnp.bfloat16
        )
        keys_values = lax.all_gather(projected[:, features:], "tensor", axis=0, tiled=True)
        attn_probs = attend(
            split_heads(projected[:, :features]), split_heads(keys_values[:, :features]), allowed
        )
        mixed_heads = jnp.einsum(
            "hqk,khd->qhd",
            attn_probs.astype(jnp.bfloat16),
            split_heads(keys_values[:, features:]),
            preferred_element_type=jnp.float32,
        )
        mixed_heads = mixed_heads.reshape(rows_own, features).astype(jnp.bfloat16)
        middle = inputs + jnp.dot(mixed_heads, out_full, preferred_element_type=jnp.float32)
        normed_two = norm_rows(middle, gains_full[1]).astype(jnp.bfloat16)
        normed_all = lax.all_gather(normed_two, "tensor", axis=0, tiled=True)
        pre_act = jnp.dot(normed_all, up_local, preferred_element_type=jnp.float32)
        hidden = gelu_tanh(pre_act).astype(jnp.bfloat16)
        branch = lax.psum_scatter(
            jnp.dot(hidden, down_local, preferred_element_type=jnp.float32).astype(jnp.bfloat16),
            "tensor",
            scatter_dimension=0,
            tiled=True,
        ).astype(jnp.float32)
        stored = (
            inputs,
            middle,
            normed_one,
            projected,
            keys_values,
            mixed_heads,
            normed_all,
            pre_act,
            hidden,
            allowed,
        )
        return (middle + branch, stored)

    def backward_layer(out_grad, stored):
        (
            inputs,
            middle,
            normed_one,
            projected,
            keys_values,
            mixed_heads,
            normed_all,
            pre_act,
            hidden,
            allowed,
        ) = stored
        out_low = out_grad.astype(jnp.bfloat16)
        out_all = lax.all_gather(out_low, "tensor", axis=0, tiled=True)
        hidden_grad = contract_last(out_all, down_local)
        pre_grad = jax.vjp(gelu_tanh, pre_act)[1](hidden_grad)[0].astype(jnp.bfloat16)
        normed_two_grad = lax.psum_scatter(
            contract_last(pre_grad, up_local).astype(jnp.bfloat16),
            "tensor",
            scatter_dimension=0,
            tiled=True,
        ).astype(jnp.float32)
        middle_back = jax.vjp(norm_rows, middle, gains_full[1])[1]
        middle_part, gain_two = middle_back(normed_two_grad)
        middle_grad = out_grad + middle_part
        branch_grad = middle_grad.astype(jnp.bfloat16)
        mixed_grad = contract_last(branch_grad, out_full).astype(jnp.bfloat16)
        query_heads = split_heads(projected[:, :features])
        key_heads = split_heads(keys_values[:, :features])
        value_heads = split_heads(keys_values[:, features:])
        attn_probs = attend(query_heads, key_heads, allowed)
        mixed_grad_heads = split_heads(mixed_grad)
        probs_grad = jnp.einsum(
            "qhd,khd->hqk", mixed_grad_heads, value_heads, preferred_element_type=jnp.float32
        )
        score_grad = attn_probs * (
            probs_grad - jnp.sum(attn_probs * probs_grad, axis=-1, keepdims=True)
        )
        score_grad = score_grad.astype(jnp.bfloat16)
        query_grad = jnp.einsum(
            "hqk,khd->qhd", score_grad, key_heads, preferred_element_type=jnp.float32
        ) * HEAD_DIM ** (-0.5)
        key_grad = jnp.einsum(
            "hqk,qhd->khd", score_grad, query_heads, preferred_element_type=jnp.float32
        ) * HEAD_DIM ** (-0.5)
        value_grad = jnp.einsum(
            "hqk,qhd->khd",
            attn_probs.astype(jnp.bfloat16),
            mixed_grad_heads,
            preferred_element_type=jnp.float32,
        )
        pair_part = jnp.concatenate(
            [key_grad.reshape(seq_rows, features), value_grad.reshape(seq_rows, features)], axis=1
        )
        pair_grad = lax.psum_scatter(
            pair_part.astype(jnp.bfloat16), "tensor", scatter_dimension=0, tiled=True
        ).astype(jnp.float32)
        projected_grad = jnp.concatenate(
            [query_grad.reshape(rows_own, features), pair_grad], axis=1
        ).astype(jnp.bfloat16)
        normed_one_grad = contract_last(projected_grad, qkv_full)
        inputs_back = jax.vjp(norm_rows, inputs, gains_full[0])[1]
        inputs_part, gain_one = inputs_back(normed_one_grad)
        weight_part = (
            normed_one,
            projected_grad,
            mixed_heads,
            branch_grad,
            normed_all,
            pre_grad,
            hidden,
            out_all,
            jnp.stack([gain_one, gain_two]),
        )
        return (middle_grad + inputs_part, weight_part)

    def run_forward(inputs, allowed):
        return forward_layer(inputs, allowed)

    def run_backward(out_grad, stored):
        return backward_layer(out_grad, stored)

    def choose(zero_side, one_side):
        return jax.tree.map(
            lambda left, right: jnp.where(is_first, left, right), zero_side, one_side
        )

    incoming = jnp.zeros((rows_own, features), jnp.bfloat16)
    kept = []
    sent = []
    for moment in range(batches + 1):
        zero_batch = min(moment, batches - 1)
        one_batch = max(moment - 1, 0)
        inputs = jnp.where(is_first, tokens[zero_batch], incoming).astype(jnp.float32)
        allowed = jnp.where(is_first, masks[zero_batch], masks[one_batch])
        if moment == 0:
            result, stored = run_forward(inputs, allowed)
        elif moment == batches:
            result, stored = run_forward(inputs, allowed)
        else:
            result, stored = forward_layer(inputs, allowed)
        result_low = result.astype(jnp.bfloat16)
        if moment < batches:
            incoming = passed_along(result_low, "section", 1)
        kept.append(stored)
        sent.append(result_low)
    activations = jnp.stack([choose(sent[which], sent[which + 1]) for which in range(batches)])
    returning = jnp.zeros((rows_own, features), jnp.bfloat16)
    back_sent = []
    parts_kept = []
    for moment in range(batches + 1):
        one_batch = min(moment, batches - 1)
        zero_batch = max(moment - 1, 0)
        stored = choose(kept[zero_batch], kept[one_batch + 1])
        upstream = jnp.where(is_first, returning, cotangent[one_batch]).astype(jnp.float32)
        if moment == 0:
            in_grad, weight_part = run_backward(upstream, stored)
        elif moment == batches:
            in_grad, weight_part = run_backward(upstream, stored)
        else:
            in_grad, weight_part = backward_layer(upstream, stored)
        grad_low = in_grad.astype(jnp.bfloat16)
        if moment < batches:
            returning = passed_along(grad_low, "section", -1)
        back_sent.append(grad_low)
        parts_kept.append(weight_part)
    input_grads = jnp.stack(
        [choose(back_sent[which + 1], back_sent[which]) for which in range(batches)]
    )
    chosen = [choose(parts_kept[which + 1], parts_kept[which]) for which in range(batches)]

    def joined(member):
        return jnp.concatenate([entry[member] for entry in chosen], axis=0)

    grad_qkv = contract_first(joined(0), joined(1))
    grad_out = contract_first(joined(2), joined(3))
    grad_up = contract_first(joined(4), joined(5))
    grad_down = contract_first(joined(6), joined(7))
    grad_gains = jnp.sum(jnp.stack([entry[8] for entry in chosen]), axis=0)
    part_qkv, part_out, part_gains = (
        lax.psum_scatter(
            grad_qkv.astype(jnp.bfloat16), "tensor", scatter_dimension=0, tiled=True
        ).astype(jnp.float32),
        lax.psum_scatter(
            grad_out.astype(jnp.bfloat16), "tensor", scatter_dimension=0, tiled=True
        ).astype(jnp.float32),
        lax.psum_scatter(
            grad_gains.astype(jnp.bfloat16), "tensor", scatter_dimension=1, tiled=True
        ).astype(jnp.float32),
    )
    share_qkv, share_out, share_gains, share_up, share_down = (
        lax.psum(part_qkv.astype(jnp.bfloat16), "dp").astype(jnp.float32),
        lax.psum(part_out.astype(jnp.bfloat16), "dp").astype(jnp.float32),
        lax.psum(part_gains.astype(jnp.bfloat16), "dp").astype(jnp.float32),
        lax.psum(grad_up.astype(jnp.bfloat16), "dp").astype(jnp.float32),
        lax.psum(grad_down.astype(jnp.bfloat16), "dp").astype(jnp.float32),
    )
    return (
        activations[None],
        input_grads[None],
        share_gains[None],
        share_qkv[None],
        share_out[None],
        share_up[None],
        share_down[None],
    )


def solution(mesh):
    placed = (
        P("dp", "tensor", None),
        P("dp", "tensor", None),
        P("dp", None),
        P("section", None, "tensor"),
        P("section", "tensor", None),
        P("section", "tensor", None),
        P("section", None, "tensor"),
        P("section", "tensor", None),
    )
    return jax.shard_map(
        body,
        mesh=mesh,
        in_specs=placed,
        out_specs=(
            P("section", "dp", "tensor", None),
            P("section", "dp", "tensor", None),
            P("section", None, "tensor"),
            P("section", "tensor", None),
            P("section", "tensor", None),
            P("section", None, "tensor"),
            P("section", "tensor", None),
        ),
        check_vma=False,
    )
```

profile of v0, /device:TPU:0, one launch (start us, length us, event | category | flops | bytes accessed | tf_op | source)
XLA Modules:
  0.0 937.0 jit_solution(15211056692642778129)
XLA Ops:
  8.2 13.3 %all-gather = bf16[1,2,1088]{1,0,2:T(2,128)(2,1)S(1)} all-gather(bf16[1,2,272]{1,0,2:T(2,128)(2,1)S(1)} %copy.276), channel_id=2, replica_groups=mesh['section'=2,'dp'=16,'tensor'=4] {'tensor'}, dimensions={2}, use_global_device_ids=true | all-gather | bytes 5440 | tf_op jit(solution)/shard_map/all_gather | solution.py:63
  23.2 19.0 %slice_reduce_fusion = (f32[1088]{0:T(1024)S(1)}, f32[1088]{0:T(1024)S(1)}) fusion(f32[1,2,1088]{1,0,2:T(1,128)} %convert_element_type.319), kind=kLoop, calls=%fused_computation.236 | loop fusion | bytes 17408 | tf_op jit(solution)/shard_map/slice | solution.py:98
  42.1 43.6 %all-gather.16.cloned.1.call-done = bf16[1,1088,3264]{2,1,0:T(8,128)(2,1)} async-done(((bf16[1,272,3264]{2,1,0:T(8,128)(2,1)}), bf16[1,1088,3264]{2,1,0:T(8,128)(2,1)}) %all-gather.16.cloned.1.call-update) | async-done | bytes 7102480 | tf_op jit(solution)/shard_map/all_gather | solution.py:61
  85.8 4.5 fusion.20
  95.6 24.7 %all-gather.10.cloned.1.call-done = bf16[384,2176]{1,0:T(8,128)(2,1)} async-done(((bf16[96,2176]{1,0:T(8,128)(2,1)}), bf16[384,2176]{1,0:T(8,128)(2,1)}) %all-gather.10.cloned.1.call-update) | async-done | bytes 1671184 | tf_op jit(solution)/shard_map/all_gather | solution.py:86
  120.3 3.0 fusion.284
  127.8 3.7 fusion.285
  131.4 3.6 fusion.169
  135.0 21.2 %all-gather.18.cloned.1.call-done = bf16[1,1088,1088]{2,1,0:T(8,128)(2,1)} async-done(((bf16[1,272,1088]{2,1,0:T(8,128)(2,1)}), bf16[1,1088,1088]{2,1,0:T(8,128)(2,1)}) %all-gather.18.cloned.1.call-update) | async-done | bytes 2367504 | tf_op jit(solution)/shard_map/all_gather | solution.py:62
  159.1 14.5 %all_gather.40 = bf16[384,1088]{1,0:T(8,128)(2,1)S(1)} all-gather(bf16[96,1088]{1,0:T(8,128)(2,1)S(1)} %multiply_convert_fusion.8), channel_id=1, replica_groups=mesh['section'=2,'dp'=16,'tensor'=4] {'tensor'}, dimensions={0}, use_global_device_ids=true | all-gather | bytes 1044480 | tf_op jit(solution)/shard_map/all_gather | solution.py:99
  179.9 22.5 %reduce-scatter.15.cloned.1.call-done = bf16[96,1088]{1,0:T(8,128)(2,1)} async-done(((bf16[384,1088]{1,0:T(8,128)(2,1)}), bf16[96,1088]{1,0:T(8,128)(2,1)}) %reduce-scatter.15.cloned.1.call-update) | async-done | bytes 208912 | tf_op jit(solution)/shard_map/reduce_scatter | solution.py:102
  206.6 4.5 fusion.23
  213.9 16.9 %all-gather.3 = bf16[1,384,1088]{2,1,0:T(8,128)(2,1)} all-gather(bf16[1,96,1088]{2,1,0:T(8,128)(2,1)S(1)} %slice_select_fusion), channel_id=5, replica_groups=mesh['section'=2,'dp'=16,'tensor'=4] {'tensor'}, dimensions={1}, use_global_device_ids=true | all-gather | bytes 1044480 | tf_op jit(solution)/shard_map/all_gather | solution.py:136
  235.3 6.4 all-gather.12.cloned.1.call-done
  241.7 3.0 fusion.283
  249.1 3.7 fusion.287
  252.8 2.8 fusion.168
  258.3 14.2 %all_gather.42 = bf16[384,1088]{1,0:T(8,128)(2,1)S(1)} all-gather(bf16[96,1088]{1,0:T(8,128)(2,1)S(1)} %get-tuple-element.101), channel_id=1, replica_groups=mesh['section'=2,'dp'=16,'tensor'=4] {'tensor'}, dimensions={0}, use_global_device_ids=true | all-gather | bytes 1044480 | tf_op jit(solution)/shard_map/all_gather | solution.py:99
  290.4 4.9 convolution_convert_fusion.8
  295.6 4.4 fusion.289
  299.9 4.1 reduce-scatter.21.cloned.1.call-done
  312.2 3.0 multiply_reduce_fusion.2
  320.5 3.3 convolution_convert_fusion.12
  326.0 3.1 pad_maximum_fusion
  333.1 2.9 fusion.164
  338.3 19.7 %reduce-scatter.23.cloned.1.call-done = bf16[96,2176]{1,0:T(8,128)(2,1)} async-done(((bf16[384,2176]{1,0:T(8,128)(2,1)}), bf16[96,2176]{1,0:T(8,128)(2,1)}) %reduce-scatter.23.cloned.1.call-update) | async-done | bytes 417808 | tf_op jit(solution)/shard_map/reduce_scatter | solution.py:177
  358.0 7.2 multiply_reduce_fusion.4
  365.1 4.5 fusion.26
  385.2 19.8 %all_gather.46 = bf16[384,1088]{1,0:T(8,128)(2,1)} all-gather(bf16[96,1088]{1,0:T(8,128)(2,1)S(1)} %bitcast_select_fusion.2), channel_id=1, replica_groups=mesh['section'=2,'dp'=16,'tensor'=4] {'tensor'}, dimensions={0}, use_global_device_ids=true | all-gather | bytes 1044480 | tf_op jit(solution)/shard_map/all_gather | solution.py:136
  405.6 3.0 fusion.281
  413.0 4.3 fusion.290
  417.3 2.8 fusion.167
  422.5 14.4 %all_gather.44 = bf16[384,1088]{1,0:T(8,128)(2,1)S(1)} all-gather(bf16[96,1088]{1,0:T(8,128)(2,1)S(1)} %get-tuple-element.97), channel_id=1, replica_groups=mesh['section'=2,'dp'=16,'tensor'=4] {'tensor'}, dimensions={0}, use_global_device_ids=true | all-gather | bytes 1044480 | tf_op jit(solution)/shard_map/all_gather | solution.py:99
  437.0 3.7 select_select_fusion.1
  446.5 3.9 broadcast_select_fusion
  457.7 3.8 fusion.292
  461.5 7.5 reduce-scatter.25.cloned.1.call-done
  478.5 3.3 convolution_convert_fusion.11
  490.2 3.1 pad_maximum_fusion.1
  493.3 2.9 fusion.165
  498.0 21.3 %reduce-scatter.27.cloned.1.call-done = bf16[96,2176]{1,0:T(8,128)(2,1)} async-done(((bf16[384,2176]{1,0:T(8,128)(2,1)}), bf16[96,2176]{1,0:T(8,128)(2,1)}) %reduce-scatter.27.cloned.1.call-update) | async-done | bytes 417808 | tf_op jit(solution)/shard_map/reduce_scatter | solution.py:177
  519.3 5.9 multiply_reduce_fusion.5
  530.7 14.9 %all_gather.47 = bf16[384,1088]{1,0:T(8,128)(2,1)S(1)} all-gather(bf16[96,1088]{1,0:T(8,128)(2,1)S(1)} %bitcast_select_fusion.1), channel_id=1, replica_groups=mesh['section'=2,'dp'=16,'tensor'=4] {'tensor'}, dimensions={0}, use_global_device_ids=true | all-gather | bytes 1044480 | tf_op jit(solution)/shard_map/all_gather | solution.py:136
  545.7 3.7 broadcast_select_fusion.5
  553.6 3.0 fusion.279
  562.3 3.8 fusion.293
  566.0 8.4 reduce-scatter.29.cloned.1.call-done
  583.3 3.3 convolution_convert_fusion.10
  594.9 3.1 pad_maximum_fusion.2
  604.7 3.4 convolution_convert_fusion.1
  609.9 2.9 fusion.166
  614.0 10.2 %reduce-scatter.31.cloned.1.call-done = bf16[96,2176]{1,0:T(8,128)(2,1)} async-done(((bf16[384,2176]{1,0:T(8,128)(2,1)}), bf16[96,2176]{1,0:T(8,128)(2,1)}) %reduce-scatter.31.cloned.1.call-update) | async-done | bytes 417808 | tf_op jit(solution)/shard_map/reduce_scatter | solution.py:177
  626.3 5.1 convolution_convert_fusion
  632.0 4.8 convolution_convert_fusion.7
  636.8 3.2 select_select_fusion.3
  642.5 3.8 fusion.19
  646.3 6.4 multiply_reduce_fusion.3
  654.0 5.9 fusion.18
  659.8 73.8 %reduce-scatter.33.cloned.1.call-done = bf16[272,3264]{1,0:T(8,128)(2,1)} async-done(((bf16[1088,3264]{1,0:T(8,128)(2,1)}), bf16[272,3264]{1,0:T(8,128)(2,1)}) %reduce-scatter.33.cloned.1.call-update) | async-done | bytes 1775632 | tf_op jit(solution)/shard_map/reduce_scatter | solution.py:263
  733.7 25.4 %reduce-scatter.19.cloned.1.call-done = bf16[96,1088]{1,0:T(8,128)(2,1)} async-done(((bf16[384,1088]{1,0:T(8,128)(2,1)}), bf16[96,1088]{1,0:T(8,128)(2,1)}) %reduce-scatter.19.cloned.1.call-update) | async-done | bytes 208912 | tf_op jit(solution)/shard_map/reduce_scatter | solution.py:102
  763.4 18.3 %reduce-scatter.37.cloned.1.call-done = bf16[272,2]{1,0:T(8,128)(2,1)} async-done(((bf16[1088,2]{1,0:T(8,128)(2,1)}), bf16[272,2]{1,0:T(8,128)(2,1)}) %reduce-scatter.37.cloned.1.call-update) | async-done | bytes 1104
  782.7 42.0 %psum.35 = bf16[1,2,272]{2,1,0:T(2,128)(2,1)S(1)} all-reduce(bf16[1,2,272]{2,1,0:T(2,128)(2,1)S(1)} %bitcast.342), channel_id=1, replica_groups=mesh['section'=2,'dp'=16,'tensor'=4] {'dp'}, use_global_device_ids=true, to_apply=%region_73.74 | all-reduce | flops 544 | bytes 2176 | tf_op jit(solution)/shard_map/psum | solution.py:276
  825.2 94.2 %all-reduce.3.cloned.1.call-done = (bf16[1,272,3264]{2,1,0:T(8,128)(2,1)}, bf16[1,272,1088]{2,1,0:T(8,128)(2,1)}, bf16[1,1088,1088]{2,1,0:T(8,128)(2,1)}, bf16[1,1088,1088]{2,1,0:T(8,128)(2,1)}) async-done(((bf16[1,272,3264]{2,1,0:T(8,128)(2,1)}, bf16[1,272,1088]{2,1,0:T(8,128)(2,1)}, bf16[1,1088,1088]{2,1,0:T(8,128)(2,1)}, bf16[1,1088,1088]{2,1,0:T(8,128)(2,1)}), (bf16[1,272,3264]{2,1,0:T(8,128)(2,1)}, ...) | async-done | bytes 7102480 | tf_op jit(solution)/shard_map/psum | solution.py:274
  919.4 4.5 broadcast_in_dim.203
  (415 shorter events, 195.2 us)
Async XLA Ops:
  7.2 167.4 %copy-start = (bf16[1,1088,1088]{2,1,0:T(8,128)(2,1)S(1)}, bf16[1,1088,1088]{2,1,0:T(8,128)(2,1)}, u32[]{:S(2)}) copy-start(bf16[1,1088,1088]{2,1,0:T(8,128)(2,1)} %param.14) | copy-start | bytes 7102468
  7.2 15.6 %copy-start.6 = (bf16[2,96,1088]{2,1,0:T(8,128)(2,1)S(1)}, bf16[2,96,1088]{2,1,0:T(8,128)(2,1)}, u32[]{:S(2)}) copy-start(bf16[2,96,1088]{2,1,0:T(8,128)(2,1)} %param.8) | copy-start | bytes 1253380
  7.2 78.6 %all-gather.16.cloned.1.call-start = ((), (), s32[]{:S(2)}) async-start(), calls=%async_computation.26 | async-start | bytes 9052160 | tf_op jit(solution)/shard_map/all_gather | solution.py:61
  7.9 112.4 %all-gather.10.cloned.1.call-start = ((), (), s32[]{:S(2)}) async-start(), calls=%async_computation.12 | async-start | bytes 2088960 | tf_op jit(solution)/shard_map/all_gather | solution.py:86
  22.9 67.3 %copy-start.68 = (f32[96]{0:T(128)}, f32[96]{0:T(128)S(1)}, u32[]{:S(2)}) copy-start(f32[96]{0:T(128)S(1)} %broadcast_multiply_fusion.11) | copy-start | bytes 1156
  23.1 67.1 %copy-start.72 = (f32[96]{0:T(128)}, f32[96]{0:T(128)S(1)}, u32[]{:S(2)}) copy-start(f32[96]{0:T(128)S(1)} %add_rsqrt_fusion.5) | copy-start | bytes 1156
  92.1 64.1 %all-gather.18.cloned.1.call-start = ((), (), s32[]{:S(2)}) async-start(), calls=%async_computation.27 | async-start | bytes 3133440 | tf_op jit(solution)/shard_map/all_gather | solution.py:62
  92.8 109.5 %reduce-scatter.15.cloned.1.call-start = ((), (), s32[]{:S(2)}) async-start(), calls=%async_computation.13 | async-start | bytes 1105920 | tf_op jit(solution)/shard_map/reduce_scatter | solution.py:102
  123.3 4.4 copy-start.63
  158.7 43.6 %copy-start.7 = (f32[96,1088]{1,0:T(8,128)}, f32[96,1088]{1,0:T(8,128)S(1)}, u32[]{:S(2)}) copy-start(f32[96,1088]{1,0:T(8,128)S(1)} %get-tuple-element.113) | copy-start | bytes 1253380
  179.8 61.9 %all-gather.12.cloned.1.call-start = ((), (), s32[]{:S(2)}) async-start(), calls=%async_computation.14 | async-start | bytes 2088960 | tf_op jit(solution)/shard_map/all_gather | solution.py:86
  203.3 2.4 collective-permute-start
  205.9 5.2 copy-start.70
  206.6 4.5 copy-start.74
  212.9 91.1 %reduce-scatter.21.cloned.1.call-start = ((), (), s32[]{:S(2)}) async-start(), calls=%async_computation.18 | async-start | bytes 1105920 | tf_op jit(solution)/shard_map/reduce_scatter | solution.py:139
  244.7 4.4 copy-start.66
  281.5 47.7 %reduce-scatter.17.cloned.1.call-start = ((), (), s32[]{:S(2)}) async-start(), calls=%async_computation.15 | async-start | bytes 1105920 | tf_op jit(solution)/shard_map/reduce_scatter | solution.py:102
  284.7 4.4 copy-start.81
  295.3 62.7 %reduce-scatter.23.cloned.1.call-start = ((), (), s32[]{:S(2)}) async-start(), calls=%async_computation.19 | async-start | bytes 2088960 | tf_op jit(solution)/shard_map/reduce_scatter | solution.py:177
  304.0 4.8 copy-start.2
  308.8 6.4 copy-start.43
  308.8 3.4 copy-start.67
  329.1 76.5 %all-gather.14.cloned.1.call-start = ((), (), s32[]{:S(2)}) async-start(), calls=%async_computation.16 | async-start | bytes 2088960 | tf_op jit(solution)/shard_map/all_gather | solution.py:86
  331.1 6.7 collective-permute-start.1
  338.2 26.9 %copy-start.80 = (f32[96]{0:T(128)}, f32[96]{0:T(128)S(1)}, u32[]{:S(2)}) copy-start(f32[96]{0:T(128)S(1)} %fusion.238) | copy-start | bytes 1156
  371.4 97.5 %reduce-scatter.25.cloned.1.call-start = ((), (), s32[]{:S(2)}) async-start(), calls=%async_computation.20 | async-start | bytes 1105920 | tf_op jit(solution)/shard_map/reduce_scatter | solution.py:139
  371.5 6.3 copy-start.18
  376.5 6.9 collective-permute-start.2
  421.4 15.5 %copy-start.89 = (f32[384,1088]{1,0:T(8,128)S(1)}, f32[384,1088]{1,0:T(8,128)}, u32[]{:S(2)}) copy-start(f32[384,1088]{1,0:T(8,128)} %copy-done.88) | copy-start | bytes 5013508
  421.4 15.5 %copy-start.93 = (f32[384,1088]{1,0:T(8,128)S(1)}, f32[384,1088]{1,0:T(8,128)}, u32[]{:S(2)}) copy-start(f32[384,1088]{1,0:T(8,128)} %copy-done.91) | copy-start | bytes 5013508
  436.9 3.8 copy-start.29
  436.9 3.8 copy-start.28
  436.9 3.8 copy-start.85
  446.3 73.0 %reduce-scatter.27.cloned.1.call-start = ((), (), s32[]{:S(2)}) async-start(), calls=%async_computation.21 | async-start | bytes 2088960 | tf_op jit(solution)/shard_map/reduce_scatter | solution.py:177
  468.9 6.2 copy-start.4
  478.5 3.3 copy-start.41
  478.5 3.3 copy-start.61
  478.5 3.3 copy-start.64
  493.2 81.2 %reduce-scatter.29.cloned.1.call-start = ((), (), s32[]{:S(2)}) async-start(), calls=%async_computation.22 | async-start | bytes 1105920 | tf_op jit(solution)/shard_map/reduce_scatter | solution.py:139
  519.3 6.3 copy-start.20
  519.3 6.3 copy-start.34
  519.3 26.3 %copy-start.95 = (bf16[384,1088]{1,0:T(8,128)(2,1)S(1)}, bf16[384,1088]{1,0:T(8,128)(2,1)}, u32[]{:S(2)}) copy-start(bf16[384,1088]{1,0:T(8,128)(2,1)} %copy-done.94) | copy-start | bytes 2506756
  519.3 26.3 %copy-start.97 = (bf16[384,1088]{1,0:T(8,128)(2,1)S(1)}, bf16[384,1088]{1,0:T(8,128)(2,1)}, u32[]{:S(2)}) copy-start(bf16[384,1088]{1,0:T(8,128)(2,1)} %copy-done.96) | copy-start | bytes 2506756
  519.3 26.3 %copy-start.99 = (f32[384,1088]{1,0:T(8,128)S(1)}, f32[384,1088]{1,0:T(8,128)}, u32[]{:S(2)}) copy-start(f32[384,1088]{1,0:T(8,128)} %copy-done.98) | copy-start | bytes 5013508
  525.2 4.7 copy-start.36
  525.3 20.4 %copy-start.90 = (f32[384,1088]{1,0:T(8,128)S(1)}, f32[384,1088]{1,0:T(8,128)}, u32[]{:S(2)}) copy-start(f32[384,1088]{1,0:T(8,128)} %copy-done.88) | copy-start | bytes 5013508
  525.6 20.1 %copy-start.86 = (bf16[1,1088,1088]{2,1,0:T(8,128)(2,1)S(1)}, bf16[1,1088,1088]{2,1,0:T(8,128)(2,1)}, u32[]{:S(2)}) copy-start(bf16[1,1088,1088]{2,1,0:T(8,128)(2,1)} %param.15) | copy-start | bytes 7102468
  526.5 3.5 copy-start.58
  526.5 3.5 collective-permute-start.3
  545.6 3.7 copy-start.30
  551.8 72.3 %reduce-scatter.31.cloned.1.call-start = ((), (), s32[]{:S(2)}) async-start(), calls=%async_computation.23 | async-start | bytes 2088960 | tf_op jit(solution)/shard_map/reduce_scatter | solution.py:177
  574.5 5.5 copy-start.5
  583.3 3.3 copy-start.65
  598.0 61.8 %reduce-scatter.35.cloned.1.call-start = ((), (), s32[]{:S(2)}) async-start(), calls=%async_computation.25 | async-start | bytes 3133440 | tf_op jit(solution)/shard_map/reduce_scatter | solution.py:266
  608.2 125.5 %reduce-scatter.33.cloned.1.call-start = ((), (), s32[]{:S(2)}) async-start(), calls=%async_computation.24 | async-start | bytes 9052160 | tf_op jit(solution)/shard_map/reduce_scatter | solution.py:263
  609.9 14.2 %copy-start.42 = (bf16[96,1088]{1,0:T(8,128)(2,1)S(1)}, bf16[96,1088]{1,0:T(8,128)(2,1)}, u32[]{:S(2)}) copy-start(bf16[96,1088]{1,0:T(8,128)(2,1)} %copy.322) | copy-start | bytes 626692
  631.4 127.6 %reduce-scatter.19.cloned.1.call-start = ((), (), s32[]{:S(2)}) async-start(), calls=%async_computation.17 | async-start | bytes 1105920 | tf_op jit(solution)/shard_map/reduce_scatter | solution.py:102
  640.1 141.6 %reduce-scatter.37.cloned.1.call-start = ((), (), s32[]{:S(2)}) async-start(), calls=%async_computation.28 | async-start | bytes 348160
  642.5 3.8 copy-start.47
  653.6 265.8 %all-reduce.3.cloned.1.call-start = ((), (), s32[]{:S(2)}) async-start(), calls=%async_computation.29 | async-start | bytes 14901248 | tf_op jit(solution)/shard_map/psum | solution.py:274
  733.7 25.4 %copy-start.16 = (f32[96,1088]{1,0:T(8,128)S(1)}, f32[96,1088]{1,0:T(8,128)}, u32[]{:S(2)}) copy-start(f32[96,1088]{1,0:T(8,128)} %copy-done.15) | copy-start | bytes 1253380
  759.1 3.3 copy-start.32
  759.1 3.3 copy-start.59
  919.4 4.5 copy-start.38
  (61 other events, 105.2 us)
Sparse Core Ops, SparseCore 0:
  9.7 76.0 all-gather.15
  92.2 28.0 all-gather.9
  122.0 34.1 all-gather.17
  180.0 22.3 reduce-scatter.14
  213.0 28.5 all-gather.11
  281.6 22.3 reduce-scatter.20
  306.4 22.5 reduce-scatter.16
  332.0 25.8 reduce-scatter.22
  371.5 34.0 all-gather.13
  446.4 22.4 reduce-scatter.24
  493.4 25.8 reduce-scatter.26
  551.9 22.5 reduce-scatter.28
  598.1 25.9 reduce-scatter.30
  627.0 32.8 reduce-scatter.34
  662.2 71.3 reduce-scatter.32
  736.5 22.4 reduce-scatter.18
  761.3 20.3 reduce-scatter.36
  786.1 133.2 all-reduce.2
where the time goes:
time: 947 us; the launch traced here: 937 us
  waiting for transfers between devices  407 us (43%)
  matrix products  154 us (16%)
  blocking collectives  150 us (16%)
  local copies, waits for them, and re-layouts  121 us (13%)
  other arithmetic  81.2 us (9%)
  between operations  16 us (2%)
    psum x1, waiting for transfers between devices, body(): lax.psum(part_qkv.astype(jnp.bfloat16), 'dp').astype(jnp.float32)  94.2 us
    reduce_scatter x1, waiting for transfers between devices, body(): lax.psum_scatter(grad_qkv.astype(jnp.bfloat16), 'tensor', scatter_dimensi...  73.8 us
    all_gather x3, blocking collectives, backward_layer(): out_all = lax.all_gather(out_low, 'tensor', axis=0, tiled=True)  51.6 us
    reduce_scatter x3, waiting for transfers between devices, backward_layer(): lax.psum_scatter(pair_part.astype(jnp.bfloat16), 'tensor', scatter_dimens...  51.1 us
    reduce_scatter x3, waiting for transfers between devices, forward_layer(): lax.psum_scatter(jnp.dot(hidden, down_local, preferred_element_type=jnp.f...  47.9 us
    all_gather x1, waiting for transfers between devices, body(): lax.all_gather(w_qkv[0], 'tensor', axis=0, tiled=True)  43.6 us
    all_gather x3, blocking collectives, forward_layer(): normed_all = lax.all_gather(normed_two, 'tensor', axis=0, tiled=True)  43.2 us
    psum x1, blocking collectives, body(): lax.psum(part_gains.astype(jnp.bfloat16), 'dp').astype(jnp.float32)  42 us
  transfers between devices with their start and end apart: 22, of which 18 were waited for; matrix products, arithmetic and copies ran while one was open for 21% of the time, Pallas kernels for 0%

commit v1 on v0

v1 whole, which is shorter than its diff:
```python
import functools
import jax
import jax.numpy as jnp
from jax import lax
from jax.experimental import pallas as pl
from jax.experimental.pallas import tpu as pltpu
from jax.sharding import PartitionSpec as P

HEAD_DIM = 64
LOW = jnp.bfloat16
F32 = jnp.float32
MESH = pl.DeviceIdType.MESH


def dot_nn(left, right):
    return lax.dot_general(left, right, (((1,), (0,)), ((), ())), preferred_element_type=F32)


def dot_nt(left, right):
    return lax.dot_general(left, right, (((1,), (1,)), ((), ())), preferred_element_type=F32)


def dot_tn(left, right):
    return lax.dot_general(left, right, (((0,), (0,)), ((), ())), preferred_element_type=F32)


def places():
    me = lax.axis_index("tensor")
    return me, lax.rem(me + 1, 4), lax.rem(me + 3, 4), lax.rem(me + 2, 4)


def greet(right, left):
    barrier = pltpu.get_barrier_semaphore()
    for neighbour in (left, right):
        pl.semaphore_signal(
            barrier, inc=1, device_id={"tensor": neighbour}, device_id_type=MESH
        )
    pl.semaphore_wait(barrier, 2)


def remote(src, dst, sems, which, target):
    return pltpu.make_async_remote_copy(
        src_ref=src,
        dst_ref=dst,
        send_sem=sems[0].at[which],
        recv_sem=sems[1].at[which],
        device_id={"tensor": target},
        device_id_type=MESH,
    )


class Gather:
    def __init__(self, full, sems):
        self.full, self.sems = full, sems
        self.me, self.right, self.left, self.opposite = places()
        half = full.shape[1] // 2
        self.first, self.second = pl.ds(0, half), pl.ds(half, half)

    def copy(self, block, rows, which, target):
        part = self.full.at[block, rows]
        return remote(part, part, self.sems, which, target)

    def start(self):
        self.copy(self.me, self.first, 0, self.right).start()
        self.copy(self.me, self.second, 1, self.left).start()
        self.copy(self.me, self.second, 2, self.right).start()
        self.copy(self.me, self.first, 3, self.left).start()

    def relay(self):
        self.copy(self.left, self.first, 0, self.right).wait_recv()
        self.copy(self.left, self.first, 4, self.right).start()
        self.copy(self.right, self.second, 1, self.left).wait_recv()
        self.copy(self.right, self.second, 5, self.left).start()

    def wait_left(self):
        self.copy(self.left, self.second, 2, self.right).wait_recv()

    def wait_right(self):
        self.copy(self.right, self.first, 3, self.left).wait_recv()

    def wait_opposite(self):
        self.copy(self.opposite, self.first, 4, self.right).wait_recv()
        self.copy(self.opposite, self.second, 5, self.left).wait_recv()

    def finish(self):
        self.copy(self.me, self.first, 0, self.right).wait_send()
        self.copy(self.me, self.second, 1, self.left).wait_send()
        self.copy(self.me, self.second, 2, self.right).wait_send()
        self.copy(self.me, self.first, 3, self.left).wait_send()
        self.copy(self.left, self.first, 4, self.right).wait_send()
        self.copy(self.right, self.second, 5, self.left).wait_send()


class Scatter:
    def __init__(self, parts, landing, passing, arrived, sems):
        self.parts, self.landing, self.passing, self.arrived = parts, landing, passing, arrived
        self.sems = sems
        self.me, self.right, self.left, self.opposite = places()
        half = parts.shape[1] // 2
        self.first, self.second = pl.ds(0, half), pl.ds(half, half)

    def copy(self, which):
        parts, first, second = self.parts, self.first, self.second
        src, dst = {
            0: lambda: (parts.at[self.opposite, first], self.landing.at[0]),
            1: lambda: (parts.at[self.opposite, second], self.landing.at[1]),
            2: lambda: (parts.at[self.right, second], self.arrived.at[0, second]),
            3: lambda: (parts.at[self.left, first], self.arrived.at[1, first]),
            4: lambda: (self.passing.at[0], self.arrived.at[0, first]),
            5: lambda: (self.passing.at[1], self.arrived.at[1, second]),
        }[which]()
        target = self.left if which in (1, 3, 5) else self.right
        return remote(src, dst, self.sems, which, target)

    def start_near(self):
        self.copy(2).start()
        self.copy(3).start()

    def start_far(self):
        self.copy(0).start()
        self.copy(1).start()

    def relay(self):
        self.copy(0).wait_recv()
        self.passing[0] = (
            self.parts[self.right, self.first].astype(F32) + self.landing[0].astype(F32)
        ).astype(LOW)
        self.copy(4).start()
        self.copy(1).wait_recv()
        self.passing[1] = (
            self.parts[self.left, self.second].astype(F32) + self.landing[1].astype(F32)
        ).astype(LOW)
        self.copy(5).start()

    def result(self):
        for which in (2, 3, 4, 5):
            self.copy(which).wait_recv()
        return (
            self.parts[self.me].astype(F32)
            + self.arrived[0].astype(F32)
            + self.arrived[1].astype(F32)
        )

    def finish(self):
        for which in range(6):
            self.copy(which).wait_send()


def norm_stats(values):
    average = jnp.mean(values, axis=-1, keepdims=True)
    centered = values - average
    variance = jnp.mean(centered * centered, axis=-1, keepdims=True)
    scale = lax.rsqrt(variance + 1e-05)
    return centered * scale, scale


def norm_back(values, gain, grad):
    xhat, scale = norm_stats(values)
    scaled = grad * gain
    part = scale * (
        scaled
        - jnp.mean(scaled, axis=-1, keepdims=True)
        - xhat * jnp.mean(scaled * xhat, axis=-1, keepdims=True)
    )
    return part, jnp.sum(grad * xhat, axis=0, keepdims=True)


def gelu_tanh(values):
    inner = 0.7978845608028654 * (values + 0.044715 * values * values * values)
    return 0.5 * values * (1.0 + jnp.tanh(inner))


def gelu_slope(values):
    square = values * values
    bent = jnp.tanh(0.7978845608028654 * values * (1.0 + 0.044715 * square))
    slope = 0.7978845608028654 * (1.0 + 3.0 * 0.044715 * square)
    return 0.5 * (1.0 + bent) + 0.5 * values * (1.0 - bent * bent) * slope


def pick_copies(layer, mine, theirs, target, sem):
    def start():
        mine_here = lax.axis_index("section") == layer

        @pl.when(mine_here)
        def _():
            pltpu.make_async_copy(mine, target, sem).start()

        @pl.when(jnp.logical_not(mine_here))
        def _():
            pltpu.make_async_copy(theirs, target, sem).start()

    def wait():
        pltpu.make_async_copy(mine, target, sem).wait()

    return start, wait


def pair_columns(features):
    width = 2 * HEAD_DIM
    return [
        (start, min(width, features - start)) for start in range(0, features, width)
    ]


def head_masks(width):
    lanes = lax.broadcasted_iota(jnp.int32, (1, width), 1)
    if width == HEAD_DIM:
        return [None]
    return [lanes < HEAD_DIM, lanes >= HEAD_DIM]


def masked(values, mask):
    return values if mask is None else jnp.where(mask, values, jnp.zeros_like(values))


def attention_weights(layer, mine, theirs, target, sems):
    pairs = []
    for half in range(2):
        pairs.append(
            pick_copies(half, mine, theirs, target.at[pl.ds(2 * half, 2)], sems.at[half])
        )
    return pairs


def forward_kernel(
    layer, features, x_ref, bias_ref, gains_ref, at_mine, at_theirs, up_mine, up_theirs, down_mine,
    down_theirs, y_ref, middle_ref, one_ref, query_ref, key_ref, value_ref, mixed_ref, two_ref,
    act_ref, hidden_ref, at_w, up_w, down_w, weight_sems, parts, landing, passing, arrived,
    key_send, key_recv, value_send, value_recv, two_send, two_recv, sum_send, sum_recv,
):
    me, right, left, opposite = places()
    fetches = attention_weights(layer, at_mine, at_theirs, at_w, weight_sems)
    fetches.append(pick_copies(layer, up_mine, up_theirs, up_w, weight_sems.at[2]))
    fetches.append(pick_copies(layer, down_mine, down_theirs, down_w, weight_sems.at[3]))
    for start, _ in fetches:
        start()
    greet(right, left)
    rows = x_ref.shape[0]
    inputs = x_ref[...].astype(F32)
    xhat, _ = norm_stats(inputs)
    one_ref[...] = (xhat * gains_ref[0:1, :]).astype(LOW)
    normed_one = one_ref[...]
    fetches[0][1]()
    key_ref[me] = dot_nn(normed_one, at_w[1]).astype(LOW)
    keys = Gather(key_ref, (key_send, key_recv))
    keys.start()
    fetches[1][1]()
    value_ref[me] = dot_nn(normed_one, at_w[2]).astype(LOW)
    values = Gather(value_ref, (value_send, value_recv))
    values.start()
    query_ref[...] = dot_nn(normed_one, at_w[0]).astype(LOW)
    keys.relay()
    values.relay()
    keys.wait_left()
    keys.wait_right()
    keys.wait_opposite()
    values.wait_left()
    values.wait_right()
    values.wait_opposite()
    bias = bias_ref[...]
    for begin, width in pair_columns(features):
        columns = pl.ds(begin, width)
        queries = query_ref[:, columns]
        key_block = key_ref[:, :, columns].reshape(4 * rows, width)
        value_block = value_ref[:, :, columns].reshape(4 * rows, width)
        mixed = None
        for mask in head_masks(width):
            scores = dot_nt(masked(queries, mask), key_block) * 0.125 + bias
            raised = jnp.exp(scores - jnp.max(scores, axis=-1, keepdims=True))
            probs = raised * (1.0 / jnp.sum(raised, axis=-1, keepdims=True))
            own = dot_nn(probs.astype(LOW), value_block)
            mixed = own if mixed is None else jnp.where(mask, own, mixed)
        mixed_ref[:, columns] = mixed.astype(LOW)
    middle_ref[...] = x_ref[...].astype(F32) + dot_nn(mixed_ref[...], at_w[3])
    xhat, _ = norm_stats(middle_ref[...])
    two_ref[me] = (xhat * gains_ref[1:2, :]).astype(LOW)
    tokens = Gather(two_ref, (two_send, two_recv))
    tokens.start()
    fetches[2][1]()
    fetches[3][1]()
    sums = Scatter(parts, landing, passing, arrived, (sum_send, sum_recv))

    def feed(block):
        act_ref[block] = dot_nn(two_ref[block], up_w[...])
        hidden_ref[block] = gelu_tanh(act_ref[block]).astype(LOW)
        parts[block] = dot_nn(hidden_ref[block], down_w[...]).astype(LOW)

    feed(me)
    tokens.relay()
    tokens.wait_left()
    feed(left)
    tokens.wait_right()
    feed(right)
    sums.start_near()
    tokens.wait_opposite()
    feed(opposite)
    sums.start_far()
    sums.relay()
    y_ref[...] = (middle_ref[...] + sums.result()).astype(LOW)
    keys.finish()
    values.finish()
    tokens.finish()
    sums.finish()


def scatter_scratch(rows, features):
    return [
        pltpu.VMEM((4, rows, features), LOW),
        pltpu.VMEM((2, rows // 2, features), LOW),
        pltpu.VMEM((2, rows // 2, features), LOW),
        pltpu.VMEM((2, rows, features), LOW),
    ]


def weight_scratch(features, hidden):
    return [
        pltpu.VMEM((4, features, features), LOW),
        pltpu.VMEM((features, hidden), LOW),
        pltpu.VMEM((hidden, features), LOW),
        pltpu.SemaphoreType.DMA((4,)),
    ]


def in_vmem():
    return pl.BlockSpec(memory_space=pltpu.VMEM)


def anywhere():
    return pl.BlockSpec(memory_space=pl.ANY)


def forward_layer(layer, x, bias, gains, attention, feed):
    rows, features = x.shape
    hidden = feed[0].shape[1]
    out_shape = (
        jax.ShapeDtypeStruct((rows, features), LOW),
        jax.ShapeDtypeStruct((rows, features), F32),
        jax.ShapeDtypeStruct((rows, features), LOW),
        jax.ShapeDtypeStruct((rows, features), LOW),
        jax.ShapeDtypeStruct((4, rows, features), LOW),
        jax.ShapeDtypeStruct((4, rows, features), LOW),
        jax.ShapeDtypeStruct((rows, features), LOW),
        jax.ShapeDtypeStruct((4, rows, features), LOW),
        jax.ShapeDtypeStruct((4, rows, hidden), F32),
        jax.ShapeDtypeStruct((4, rows, hidden), LOW),
    )
    return pl.pallas_call(
        functools.partial(forward_kernel, layer, features),
        out_shape=out_shape,
        in_specs=[in_vmem()] * 3 + [anywhere()] * 6,
        out_specs=[in_vmem()] * len(out_shape),
        scratch_shapes=weight_scratch(features, hidden)
        + scatter_scratch(rows, features)
        + [pltpu.SemaphoreType.DMA((6,))] * 8,
        compiler_params=pltpu.CompilerParams(
            collective_id=layer, has_side_effects=True, vmem_limit_bytes=56 * 2**20
        ),
        cost_estimate=pl.CostEstimate(
            flops=3 * 10**9, bytes_accessed=24 * 10**6, transcendentals=10**6
        ),
        name=f"layer_forward_{layer}",
    )(x, bias, gains, *attention, *feed)


def backward_kernel(
    layer, features, x_ref, dy_ref, bias_ref, gains_ref, middle_ref, query_ref, key_ref, value_ref,
    act_ref, at_mine, at_theirs, up_mine, up_theirs, down_mine, down_theirs,
    dx_ref, gain_ref, out_ref, pre_ref, branch_ref, dquery_ref, dkey_ref, dvalue_ref,
    at_w, up_w, down_w, weight_sems, parts, landing, passing, arrived, parts_b, landing_b,
    passing_b, arrived_b, parts_c, landing_c, passing_c, arrived_c, mixed_grad,
    out_send, out_recv, sum_send, sum_recv, key_send, key_recv, value_send, value_recv,
):
    me, right, left, opposite = places()
    fetches = attention_weights(layer, at_mine, at_theirs, at_w, weight_sems)
    fetches.append(pick_copies(layer, up_mine, up_theirs, up_w, weight_sems.at[2]))
    fetches.append(pick_copies(layer, down_mine, down_theirs, down_w, weight_sems.at[3]))
    for which in (3, 2, 1, 0):
        fetches[which][0]()
    rows = x_ref.shape[0]
    out_ref[me] = dy_ref[...]
    greet(right, left)
    grads = Gather(out_ref, (out_send, out_recv))
    grads.start()
    sums = Scatter(parts, landing, passing, arrived, (sum_send, sum_recv))
    fetches[3][1]()
    fetches[2][1]()

    def feed(block):
        hidden_grad = dot_nt(out_ref[block], down_w[...])
        pre_ref[block] = (hidden_grad * gelu_slope(act_ref[block])).astype(LOW)
        parts[block] = dot_nt(pre_ref[block], up_w[...]).astype(LOW)

    feed(me)
    grads.relay()
    grads.wait_left()
    feed(left)
    grads.wait_right()
    feed(right)
    sums.start_near()
    grads.wait_opposite()
    feed(opposite)
    sums.start_far()
    sums.relay()
    middle_part, gain_two = norm_back(middle_ref[...], gains_ref[1:2, :], sums.result())
    gain_ref[1:2, :] = gain_two
    middle_grad = dy_ref[...].astype(F32) + middle_part
    middle_ref_grad = middle_grad
    branch_ref[...] = middle_grad.astype(LOW)
    fetches[1][1]()
    mixed_grad[...] = dot_nt(branch_ref[...], at_w[3]).astype(LOW)
    bias = bias_ref[...]
    for begin, width in pair_columns(features):
        columns = pl.ds(begin, width)
        queries = query_ref[:, columns]
        outer = mixed_grad[:, columns]
        key_block = key_ref[:, :, columns].reshape(4 * rows, width)
        value_block = value_ref[:, :, columns].reshape(4 * rows, width)
        dquery = dkey = dvalue = None
        for mask in head_masks(width):
            query_one, outer_one = masked(queries, mask), masked(outer, mask)
            scores = dot_nt(key_block, query_one) * 0.125 + bias
            raised = jnp.exp(scores - jnp.max(scores, axis=0, keepdims=True))
            probs = raised * (1.0 / jnp.sum(raised, axis=0, keepdims=True))
            probs_grad = dot_nt(value_block, outer_one)
            mean = jnp.sum(probs * probs_grad, axis=0, keepdims=True)
            score_grad = (probs * (probs_grad - mean)).astype(LOW)
            own_query = dot_tn(score_grad, key_block)
            own_key = dot_nn(score_grad, query_one)
            own_value = dot_nn(probs.astype(LOW), outer_one)
            if dquery is None:
                dquery, dkey, dvalue = own_query, own_key, own_value
            else:
                dquery = jnp.where(mask, own_query, dquery)
                dkey, dvalue = dkey + own_key, dvalue + own_value
        dquery_ref[:, columns] = (dquery * 0.125).astype(LOW)
        parts_b[:, :, columns] = (dkey * 0.125).astype(LOW).reshape(4, rows, width)
        parts_c[:, :, columns] = dvalue.astype(LOW).reshape(4, rows, width)
    dkeys = Scatter(parts_b, landing_b, passing_b, arrived_b, (key_send, key_recv))
    dvalues = Scatter(parts_c, landing_c, passing_c, arrived_c, (value_send, value_recv))
    dkeys.start_far()
    dvalues.start_far()
    dkeys.start_near()
    dvalues.start_near()
    fetches[0][1]()
    one_grad = dot_nt(dquery_ref[...], at_w[0])
    dkeys.relay()
    dvalues.relay()
    dkey_ref[...] = dkeys.result().astype(LOW)
    dvalue_ref[...] = dvalues.result().astype(LOW)
    one_grad = one_grad + dot_nt(dkey_ref[...], at_w[1]) + dot_nt(dvalue_ref[...], at_w[2])
    inputs_part, gain_one = norm_back(x_ref[...].astype(F32), gains_ref[0:1, :], one_grad)
    gain_ref[0:1, :] = gain_one
    dx_ref[...] = (middle_ref_grad + inputs_part).astype(LOW)
    grads.finish()
    sums.finish()
    dkeys.finish()
    dvalues.finish()


def backward_layer(layer, x, dy, bias, gains, middle, query, key, value, act, attention, feed):
    rows, features = x.shape
    hidden = feed[0].shape[1]
    out_shape = (
        jax.ShapeDtypeStruct((rows, features), LOW),
        jax.ShapeDtypeStruct((2, features), F32),
        jax.ShapeDtypeStruct((4, rows, features), LOW),
        jax.ShapeDtypeStruct((4, rows, hidden), LOW),
        jax.ShapeDtypeStruct((rows, features), LOW),
        jax.ShapeDtypeStruct((rows, features), LOW),
        jax.ShapeDtypeStruct((rows, features), LOW),
        jax.ShapeDtypeStruct((rows, features), LOW),
    )
    return pl.pallas_call(
        functools.partial(backward_kernel, layer, features),
        out_shape=out_shape,
        in_specs=[in_vmem()] * 9 + [anywhere()] * 6,
        out_specs=[in_vmem()] * len(out_shape),
        scratch_shapes=weight_scratch(features, hidden)
        + scatter_scratch(rows, features) * 3
        + [pltpu.VMEM((rows, features), LOW)]
        + [pltpu.SemaphoreType.DMA((6,))] * 8,
        compiler_params=pltpu.CompilerParams(
            collective_id=2 + layer, has_side_effects=True, vmem_limit_bytes=56 * 2**20
        ),
        cost_estimate=pl.CostEstimate(
            flops=4 * 10**9, bytes_accessed=24 * 10**6, transcendentals=10**6
        ),
        name=f"layer_backward_{layer}",
    )(x, dy, bias, gains, middle, query, key, value, act, *attention, *feed)


def doc_numbers(lengths, positions):
    doc_ends = jnp.cumsum(lengths)
    return jnp.sum((positions[:, None] >= doc_ends[None, :]).astype(jnp.int32), axis=1)


def contract_first(left, right):
    return lax.dot_general(
        left, right, (((0,), (0,)), ((), ())), preferred_element_type=F32
    )


def swapped(block):
    return lax.ppermute(block, "section", [(0, 1), (1, 0)])


def body(tokens, cotangent, doc_lengths, norm_gains, w_qkv, w_out, w_up, w_down):
    batches, rows, features = tokens.shape
    seq_rows = rows * lax.axis_size("tensor")
    section = lax.axis_index("section")
    is_first = section == 0

    def choose(zero_side, one_side):
        return jnp.where(is_first, zero_side, one_side)

    own_tokens = lax.dynamic_index_in_dim(tokens, section, 0, keepdims=False)
    own_cotangent = lax.dynamic_index_in_dim(cotangent, section, 0, keepdims=False)
    lengths = lax.dynamic_index_in_dim(doc_lengths, section, 0, keepdims=False)
    own_places = lax.axis_index("tensor") * rows + jnp.arange(rows, dtype=jnp.int32)
    all_places = jnp.arange(seq_rows, dtype=jnp.int32)
    own_docs = doc_numbers(lengths, own_places)
    all_docs = doc_numbers(lengths, all_places)
    allowed = (all_places[None, :] <= own_places[:, None]) & (
        all_docs[None, :] == own_docs[:, None]
    )
    bias = jnp.where(allowed, 0.0, -1e30).astype(F32)
    bias_turned = bias.T
    gains = lax.all_gather(
        lax.all_gather(norm_gains[0], "tensor", axis=1, tiled=True), "section", axis=0
    ).astype(F32)

    query_key = jnp.stack([w_qkv[0, :, :features], w_qkv[0, :, features : 2 * features]])
    value_out = jnp.stack([w_qkv[0, :, 2 * features :], w_out[0]])
    crossed = swapped(choose(value_out, query_key))
    zero_mine = lax.all_gather(choose(query_key, crossed), "tensor", axis=1, tiled=True)
    zero_theirs = swapped(zero_mine)
    one_mine = lax.all_gather(choose(crossed, value_out), "tensor", axis=1, tiled=True)
    one_theirs = swapped(one_mine)
    attention = ((zero_mine, zero_theirs), (one_mine, one_theirs))
    feed = (w_up[0], swapped(w_up[0]), w_down[0], swapped(w_down[0]))

    inputs = own_tokens
    saved = []
    for layer in range(2):
        results = forward_layer(layer, inputs, bias, gains[layer], attention[layer], feed)
        saved.append((inputs,) + tuple(results))
        inputs = results[0]
    activations = (saved[0][1], saved[1][1])

    grad = own_cotangent
    input_grads = [None, None]
    gain_grads = [None, None]
    feed_sums = [None, None]
    attention_sums = [None, None]
    for layer in (1, 0):
        (x, _, middle, normed_one, query, key, value, mixed, normed_two, act, hidden) = saved[layer]
        (grad, gain_grad, out_all, pre_grad, branch, dquery, dkey, dvalue) = backward_layer(
            layer, x, grad, bias_turned, gains[layer], middle, query, key, value, act,
            attention[layer], feed,
        )
        input_grads[layer] = grad
        gain_grads[layer] = gain_grad

        def flat(block):
            return block.reshape(seq_rows, block.shape[-1])

        up_left, up_right = flat(normed_two), flat(pre_grad)
        down_left, down_right = flat(hidden), flat(out_all)
        mine_left, mine_right = choose(up_left, down_left), choose(up_right, down_right)
        their_left = swapped(choose(down_left, up_left))
        their_right = swapped(choose(down_right, up_right))
        feed_grad = contract_first(mine_left, mine_right) + contract_first(their_left, their_right)
        feed_grad = feed_grad.astype(LOW)
        if layer == 0:
            feed_grad, feed_sums[1] = lax.optimization_barrier((feed_grad, feed_sums[1]))
        feed_sums[layer] = lax.psum(feed_grad, "dp")
        first_left, first_right = jnp.stack([normed_one, normed_one]), jnp.stack([dquery, dkey])
        other_left, other_right = jnp.stack([normed_one, mixed]), jnp.stack([dvalue, branch])
        left = jnp.concatenate(
            [choose(first_left, other_left), swapped(choose(other_left, first_left))], axis=1
        )
        right = jnp.concatenate(
            [choose(first_right, other_right), swapped(choose(other_right, first_right))], axis=1
        )
        attention_grad = lax.dot_general(
            left, right, (((1,), (1,)), ((0,), (0,))), preferred_element_type=F32
        ).astype(LOW)
        part = lax.psum_scatter(attention_grad, "tensor", scatter_dimension=1, tiled=True)
        if layer == 0:
            part, attention_sums[1] = lax.optimization_barrier((part, attention_sums[1]))
        attention_sums[layer] = lax.psum(part, "dp")

    gain_total = lax.psum(jnp.stack(gain_grads), ("section", "dp", "tensor"))
    gain_own = lax.dynamic_index_in_dim(gain_total, section, 0, keepdims=True)
    share = features // lax.axis_size("tensor")
    gain_own = lax.dynamic_slice_in_dim(gain_own, lax.axis_index("tensor") * share, share, 2)
    kept_activation = choose(activations[0], activations[1])
    their_activation = swapped(choose(activations[1], activations[0]))
    kept_grad = choose(input_grads[0], input_grads[1])
    their_grad = swapped(choose(input_grads[1], input_grads[0]))

    def in_order(mine, theirs):
        return jnp.stack([choose(mine, theirs), choose(theirs, mine)])[None]

    feed_kept = choose(feed_sums[0], feed_sums[1])
    feed_other = swapped(choose(feed_sums[1], feed_sums[0]))
    attention_kept = choose(attention_sums[0], attention_sums[1])
    attention_other = swapped(choose(attention_sums[1], attention_sums[0]))
    first_half = choose(attention_kept, attention_other).astype(F32)
    other_half = choose(attention_other, attention_kept).astype(F32)
    grad_qkv = jnp.concatenate([first_half[0], first_half[1], other_half[0]], axis=1)
    return (
        in_order(kept_activation, their_activation),
        in_order(kept_grad, their_grad),
        gain_own,
        grad_qkv[None],
        other_half[1][None],
        choose(feed_kept, feed_other).astype(F32)[None],
        choose(feed_other, feed_kept).astype(F32)[None],
    )


def solution(mesh):
    placed = (
        P("dp", "tensor", None),
        P("dp", "tensor", None),
        P("dp", None),
        P("section", None, "tensor"),
        P("section", "tensor", None),
        P("section", "tensor", None),
        P("section", None, "tensor"),
        P("section", "tensor", None),
    )
    return jax.shard_map(
        body,
        mesh=mesh,
        in_specs=placed,
        out_specs=(
            P("section", "dp", "tensor", None),
            P("section", "dp", "tensor", None),
            P("section", None, "tensor"),
            P("section", "tensor", None),
            P("section", "tensor", None),
            P("section", None, "tensor"),
            P("section", "tensor", None),
        ),
        check_vma=False,
    )
```

time: 947 us -> 661 us (0.70)
  Pallas kernels: 0 us -> 200 us
  matrix products: 154 us -> 19.5 us
  waiting for transfers between devices: 407 us -> 281 us
  local copies, waits for them, and re-layouts: 121 us -> 27.5 us
  blocking collectives: 150 us -> 82.2 us
  other arithmetic: 81.2 us -> 24.5 us
    pallas_call x0 -> x4, Pallas kernels: none -> 200 us  [the longest x2 102 us: backward_layer(): pl.pallas_call(functools.partial(backward_kernel, layer, features), out_s...]
    dot_general x39 -> x2, matrix products: 112 us -> 7.89 us  [body(): lax.dot_general(left, right, (((1,), (1,)), ((0,), (0,))), preferred_elem...]
    reduce_scatter x11 -> x2, waiting for transfers between devices: 193 us -> 93.6 us  [body(): lax.psum_scatter(attention_grad, 'tensor', scatter_dimension=1, tiled=True)]
    all_gather x6 -> x1, blocking collectives: 94.8 us -> 1.97 us  [body(): lax.all_gather(lax.all_gather(norm_gains[0], 'tensor', axis=1, tiled=True...]
    slice x30 -> x2, local copies, waits for them, and re-layouts: 72.3 us -> 3.47 us  [the longest x1 1.86 us: body(): w_qkv[0, :, :features]]
    psum x1 -> x2, waiting for transfers between devices: 94.2 us -> 60.4 us  [body(): attention_sums[layer] = lax.psum(part, 'dp')]
    psum x1, blocking collectives: 42 us -> 66.5 us  [body(): gain_total = lax.psum(jnp.stack(gain_grads), ('section', 'dp', 'tensor'))]
    sub x6 -> x0, matrix products: 23.6 us -> none  [attend(): raised = jnp.exp(scores - row_max)]
  transfers between devices with their start and end apart: 22 -> 23, of which waited for: 18 -> 13; matrix products, arithmetic and copies ran while one was open for 21% -> 8% of each run, Pallas kernels for 0% -> 16%
where the time goes in v1:
time: 661 us; the launch traced here: 657 us
  waiting for transfers between devices  281 us (43%)
  Pallas kernels  200 us (30%)
  blocking collectives  82.2 us (12%)
  local copies, waits for them, and re-layouts  27.5 us (4%)
  other arithmetic  24.5 us (4%)
  matrix products  19.5 us (3%)
  between operations  14.7 us (2%)
  starting transfers between devices  7.98 us (1%)
    pallas_call x2, Pallas kernels, backward_layer(): pl.pallas_call(functools.partial(backward_kernel, layer, features), out_s...  102 us
    pallas_call x2, Pallas kernels, forward_layer(): pl.pallas_call(functools.partial(forward_kernel, layer, features), out_sh...  97.9 us
    reduce_scatter x2, waiting for transfers between devices, body(): lax.psum_scatter(attention_grad, 'tensor', scatter_dimension=1, tiled=True)  93.6 us
    psum x1, blocking collectives, body(): gain_total = lax.psum(jnp.stack(gain_grads), ('section', 'dp', 'tensor'))  66.5 us
    psum x2, waiting for transfers between devices, body(): attention_sums[layer] = lax.psum(part, 'dp')  60.4 us
    all_gather x1, waiting for transfers between devices, body(): lax.all_gather(choose(crossed, value_out), 'tensor', axis=1, tiled=True)  57.8 us
    all_gather x1, waiting for transfers between devices, body(): lax.all_gather(choose(query_key, crossed), 'tensor', axis=1, tiled=True)  56.9 us
    all_gather x1, blocking collectives, body(): lax.all_gather(norm_gains[0], 'tensor', axis=1, tiled=True)  13.7 us
  transfers between devices with their start and end apart: 23, of which 13 were waited for; matrix products, arithmetic and copies ran while one was open for 8% of the time, Pallas kernels for 16%

profile of v1, /device:TPU:0, one launch (start us, length us, event | category | flops | bytes accessed | tf_op | source)
XLA Modules:
  0.0 656.7 jit_solution(5000456981652273882)
XLA Ops:
  7.2 1.9 fusion.30
  9.5 2.9 collective-permute-done
  12.5 1.9 broadcast_select_fusion.4
  14.4 0.7 all-gather.7.cloned.1.call-update
  15.2 56.9 %all-gather.5.cloned.1.call-done.at_mine = bf16[2,1088,1088]{2,1,0:T(8,128)(2,1)} async-done(((bf16[2,272,1088]{2,1,0:T(8,128)(2,1)}), bf16[2,1088,1088]{2,1,0:T(8,128)(2,1)}) %all-gather.5.cloned.1.call-update) | async-done | bytes 4734992 | tf_op jit(solution)/shard_map/all_gather | solution.py:535
  72.0 57.8 %all-gather.7.cloned.1.call-done.at_mine = bf16[2,1088,1088]{2,1,0:T(8,128)(2,1)} async-done(((bf16[2,272,1088]{2,1,0:T(8,128)(2,1)}), bf16[2,1088,1088]{2,1,0:T(8,128)(2,1)}) %all-gather.7.cloned.1.call-update) | async-done | bytes 4734992 | tf_op jit(solution)/shard_map/all_gather | solution.py:537
  130.5 0.8 copy.21
  131.4 13.7 %all-gather = bf16[1,2,1088]{1,0,2:T(2,128)(2,1)S(1)} all-gather(bf16[1,2,272]{1,0,2:T(2,128)(2,1)} %copy.21), channel_id=2, replica_groups=mesh['section'=2,'dp'=16,'tensor'=4] {'tensor'}, dimensions={2}, use_global_device_ids=true | all-gather | bytes 5440 | tf_op jit(solution)/shard_map/all_gather | solution.py:529
  145.1 0.7 copy.22
  145.8 2.0 all-gather.1
  148.0 0.8 fusion.25.bias_ref
  148.8 0.8 fusion.23.bias_ref
  149.6 0.7 dynamic-slice_bitcast_fusion.1.x_ref
  150.3 1.6 dynamic-slice_bitcast_fusion.dy_ref
  151.9 0.6 slice_bitcast_fusion.3
  152.5 50.7 %layer_forward_0.1 = (bf16[96,1088]{1,0:T(8,128)(2,1)}, f32[96,1088]{1,0:T(8,128)}, bf16[96,1088]{1,0:T(8,128)(2,1)}, bf16[96,1088]{1,0:T(8,128)(2,1)}, bf16[4,9...) custom-call(bf16[96,1088]{1,0:T(8,128)(2,1)} %dynamic-slice_bitcast_, ...), custom_call_target="tpu_custom_call" | custom-call | flops 3000000000 | bytes 24000000 | tf_op jit(solution)/shard_map/layer_forward_0/pallas_call | solution.py:347
  203.2 47.2 %layer_forward_1.1 = (bf16[96,1088]{1,0:T(8,128)(2,1)}, f32[96,1088]{1,0:T(8,128)}, bf16[96,1088]{1,0:T(8,128)(2,1)}, bf16[96,1088]{1,0:T(8,128)(2,1)}, bf16[4,9...) custom-call(bf16[96,1088]{1,0:T(8,128)(2,1)} %get-tuple-element.47.x, ...), custom_call_target="tpu_custom_call" | custom-call | flops 3000000000 | bytes 24000000 | tf_op jit(solution)/shard_map/layer_forward_1/pallas_call | solution.py:347
  250.4 48.4 %layer_backward_1.1 = (bf16[96,1088]{1,0:T(8,128)(2,1)}, f32[2,1088]{1,0:T(2,128)}, bf16[4,96,1088]{2,1,0:T(8,128)(2,1)}, bf16[4,96,1088]{2,1,0:T(8,128)(2,1)}, ...) custom-call(bf16[96,1088]{1,0:T(8,128)(2,1)} %get-tuple-element.47.x_r, ...), custom_call_target="tpu_custom_call" | custom-call | flops 4000000000 | bytes 24000000 | tf_op jit(solution)/shard_map/layer_backward_1/pallas_call | solution.py:473
  298.9 1.4 broadcast_select_fusion.12
  300.5 0.6 collective-permute-start.9
  301.1 1.1 collective-permute-done.10
  302.2 0.6 collective-permute-done.9
  302.8 3.9 convolution_convert_fusion
  306.8 1.1 copy-done.13
  307.9 1.0 broadcast_select_fusion.7
  308.9 2.2 copy.26
  311.1 1.4 collective-permute-start.15
  312.6 1.0 broadcast_select_fusion.10
  313.6 2.2 copy.25
  315.8 2.6 collective-permute-done.14
  318.3 2.7 fusion.32
  321.1 3.1 fusion.3
  324.2 37.9 %reduce-scatter.5.cloned.1.call-done = bf16[2,272,1088]{2,1,0:T(8,128)(2,1)} async-done(((bf16[2,1088,1088]{2,1,0:T(8,128)(2,1)}), bf16[2,272,1088]{2,1,0:T(8,128)(2,1)}) %reduce-scatter.5.cloned.1.call-update) | async-done | bytes 1183760 | tf_op jit(solution)/shard_map/reduce_scatter | solution.py:588
  362.6 53.2 %layer_backward_0.1 = (bf16[96,1088]{1,0:T(8,128)(2,1)}, f32[2,1088]{1,0:T(2,128)}, bf16[4,96,1088]{2,1,0:T(8,128)(2,1)}, bf16[4,96,1088]{2,1,0:T(8,128)(2,1)}, ...) custom-call(bf16[96,1088]{1,0:T(8,128)(2,1)} %dynamic-slice_bitcast_fu, ...), custom_call_target="tpu_custom_call" | custom-call | flops 4000000000 | bytes 24000000 | tf_op jit(solution)/shard_map/layer_backward_0/pallas_call | solution.py:473
  415.8 1.4 broadcast_select_fusion.16
  417.5 0.6 collective-permute-start.7
  418.1 1.1 collective-permute-done.8
  419.2 0.6 collective-permute-done.7
  419.8 3.9 convolution_convert_fusion.1
  423.8 1.1 copy-done.11
  424.9 1.0 broadcast_select_fusion.8
  426.0 2.2 copy.24
  428.2 1.4 collective-permute-start.13
  429.6 1.0 broadcast_select_fusion.9
  430.6 2.2 copy.23
  432.8 2.6 collective-permute-done.12
  435.4 2.7 fusion.31
  438.1 3.1 fusion.2
  441.2 25.2 %all-reduce.7.cloned.1.call-done = (bf16[2,272,1088]{2,1,0:T(8,128)(2,1)}, bf16[1088,1088]{1,0:T(8,128)(2,1)}) async-done(((bf16[2,272,1088]{2,1,0:T(8,128)(2,1)}, bf16[1088,1088]{1,0:T(8,128)(2,1)}), (bf16[2,272,1088]{2,1,0:T(8,128)(2,1)}, bf16[1088,1088]{1,0:T(8,128)(2,1)})) %all-reduce.7.cloned.1.call-update) | async-done | bytes 3551248 | tf_op jit(solution)/shard_map/psum | solution.py:591
  466.4 55.7 %reduce-scatter.3.cloned.1.call-done = bf16[2,272,1088]{2,1,0:T(8,128)(2,1)} async-done(((bf16[2,1088,1088]{2,1,0:T(8,128)(2,1)}), bf16[2,272,1088]{2,1,0:T(8,128)(2,1)}) %reduce-scatter.3.cloned.1.call-update) | async-done | bytes 1183760 | tf_op jit(solution)/shard_map/reduce_scatter | solution.py:588
  522.1 0.9 copy-done.16
  523.9 66.5 %psum.35 = f32[2,2,1088]{2,1,0:T(2,128)S(1)} all-reduce(f32[2,2,1088]{2,1,0:T(2,128)S(1)} %pad_maximum_fusion.10), channel_id=1, replica_groups=mesh['section'=2,'dp'=16,'tensor'=4] {'section','dp','tensor'}, use_global_device_ids=true, to_apply=%region_3.4 | all-reduce | flops 4352 | bytes 34816 | tf_op jit(solution)/shard_map/psum | solution.py:593
  590.3 0.7 constant_dynamic-slice_fusion
  591.1 0.7 select_bitcast_fusion.3
  591.8 35.2 %all-reduce.5.cloned.1.call-done = (bf16[2,272,1088]{2,1,0:T(8,128)(2,1)}, bf16[1088,1088]{1,0:T(8,128)(2,1)}) async-done(((bf16[2,272,1088]{2,1,0:T(8,128)(2,1)}, bf16[1088,1088]{1,0:T(8,128)(2,1)}), (bf16[2,272,1088]{2,1,0:T(8,128)(2,1)}, bf16[1088,1088]{1,0:T(8,128)(2,1)})) %all-reduce.5.cloned.1.call-update) | async-done | bytes 3551248 | tf_op jit(solution)/shard_map/psum | solution.py:591
  627.0 1.6 broadcast_select_fusion.2
  629.1 1.7 broadcast_select_fusion
  630.8 1.9 collective-permute-start.16
  632.7 0.8 maximum_bitcast_fusion.1
  633.5 0.8 maximum_bitcast_fusion
  634.7 1.6 fusion.29
  636.3 1.7 slice_bitcast_fusion.1
  638.0 4.6 concatenate.19
  642.6 7.1 %bitcast_convert_fusion = (f32[1,1088,1088]{2,1,0:T(8,128)}, f32[1,1088,1088]{2,1,0:T(8,128)}) fusion(bf16[1088,1088]{1,0:T(8,128)(2,1)} %collective-permute-done.16, pred[]{:T(512)S(6)} %eq.23, bf16[1088,1088]{1,0:T(8,128)(2,1)} %get-tuple-element.88, bf16[1088,1088]{1,0:T(8,128)(2,1)S(1)} %copy-done.3), kind=kLoop, calls=%fused_computation.8 | loop fusion | flops 5918720 | bytes 16572417 | tf_op jit(solution)/shard_map/broadcast_in_dim | solution.py:619
  (100 shorter events, 4.2 us)
Async XLA Ops:
  7.2 142.4 %copy-start = (bf16[2,96,1088]{2,1,0:T(8,128)(2,1)S(1)}, bf16[2,96,1088]{2,1,0:T(8,128)(2,1)}, u32[]{:S(2)}) copy-start(bf16[2,96,1088]{2,1,0:T(8,128)(2,1)} %param.8) | copy-start | bytes 1253380
  7.2 64.8 %all-gather.5.cloned.1.call-start = ((), (), s32[]{:S(2)}) async-start(), calls=%async_computation.2 | async-start | bytes 6266880 | tf_op jit(solution)/shard_map/all_gather | solution.py:535
  7.2 1.9 copy-start.15
  9.4 3.0 collective-permute-start
  14.3 115.5 %copy-start.2 = (bf16[1,1088,1088]{2,1,0:T(8,128)(2,1)S(1)}, bf16[1,1088,1088]{2,1,0:T(8,128)(2,1)}, u32[]{:S(2)}) copy-start(bf16[1,1088,1088]{2,1,0:T(8,128)(2,1)} %param.14) | copy-start | bytes 7102468
  14.3 116.0 %copy-start.27 = (s32[2,4]{1,0:T(2,128)S(1)}, s32[2,4]{1,0:T(2,128)}, u32[]{:S(2)}) copy-start(s32[2,4]{1,0:T(2,128)} %param.10) | copy-start | bytes 100
  14.3 116.2 %copy-start.26 = (bf16[1,2,272]{2,1,0:T(2,128)(2,1)S(1)}, bf16[1,2,272]{2,1,0:T(2,128)(2,1)}, u32[]{:S(2)}) copy-start(bf16[1,2,272]{2,1,0:T(2,128)(2,1)} %param.11) | copy-start | bytes 3268
  14.4 115.4 %all-gather.7.cloned.1.call-start = ((), (), s32[]{:S(2)}) async-start(), calls=%async_computation.3 | async-start | bytes 6266880 | tf_op jit(solution)/shard_map/all_gather | solution.py:537
  15.1 347.0 %reduce-scatter.5.cloned.1.call-start = ((), (), s32[]{:S(2)}) async-start(), calls=%async_computation.5 | async-start | bytes 6266880 | tf_op jit(solution)/shard_map/reduce_scatter | solution.py:588
  72.0 80.5 %collective-permute-start.1 = (bf16[2,1088,1088]{2,1,0:T(8,128)(2,1)}, bf16[2,1088,1088]{2,1,0:T(8,128)(2,1)}, u32[]{:S(2)}, u32[]{:S(2)}) collective-permute-start(bf16[2,1088,1088]{2,1,0:T(8,128)(2,1)} %all-gather.5.cloned.1.call-done.at_mine), channel_id=1, source_target_pairs={{0,64},{64,0},{1,65},{65,1},{2,66},{66,2},{3,67},{67,3},{4,68},{68... | collective-permute-start | bytes 14204936 | tf_op jit(solution)/shard_map/ppermute | solution.py:504
  129.8 73.4 %collective-permute-start.4 = (bf16[2,1088,1088]{2,1,0:T(8,128)(2,1)}, bf16[2,1088,1088]{2,1,0:T(8,128)(2,1)}, u32[]{:S(2)}, u32[]{:S(2)}) collective-permute-start(bf16[2,1088,1088]{2,1,0:T(8,128)(2,1)} %all-gather.7.cloned.1.call-done.at_mine), channel_id=1, source_target_pairs={{0,64},{64,0},{1,65},{65,1},{2,66},{66,2},{3,67},{67,3},{4,68},{68... | collective-permute-start | bytes 14204936 | tf_op jit(solution)/shard_map/ppermute | solution.py:504
  129.8 22.7 %collective-permute-start.2 = (bf16[1088,1088]{1,0:T(8,128)(2,1)S(1)}, bf16[1088,1088]{1,0:T(8,128)(2,1)}, u32[]{:S(2)}, u32[]{:S(2)}) collective-permute-start(bf16[1088,1088]{1,0:T(8,128)(2,1)S(1)} %bitcast.76), channel_id=1, source_target_pairs={{0,64},{64,0},{1,65},{65,1},{2,66},{66,2},{3,67},{67,3},{4,68},{68... | collective-permute-start | bytes 7102472 | tf_op jit(solution)/shard_map/ppermute | solution.py:504
  130.3 22.2 %collective-permute-start.3 = (bf16[1088,1088]{1,0:T(8,128)(2,1)}, bf16[1088,1088]{1,0:T(8,128)(2,1)}, u32[]{:S(2)}, u32[]{:S(2)}) collective-permute-start(bf16[1088,1088]{1,0:T(8,128)(2,1)} %bitcast.77), channel_id=1, source_target_pairs={{0,64},{64,0},{1,65},{65,1},{2,66},{66,2},{3,67},{67,3},{4,68},{68... | collective-permute-start | bytes 7102472 | tf_op jit(solution)/shard_map/ppermute | solution.py:504
  298.8 1.6 copy-start.22
  298.8 1.6 copy-start.23
  300.3 1.9 collective-permute-start.10
  300.5 2.3 collective-permute-start.9
  306.8 1.2 copy-start.13
  306.8 159.6 %all-reduce.7.cloned.1.call-start = ((), (), s32[]{:S(2)}) async-start(), calls=%async_computation.7 | async-start | bytes 7520256 | tf_op jit(solution)/shard_map/psum | solution.py:591
  307.9 4.6 copy-start.9
  307.9 4.6 copy-start.10
  311.1 4.6 collective-permute-start.15
  315.8 5.3 copy-start.14
  315.8 2.6 collective-permute-start.14
  362.1 159.9 %reduce-scatter.3.cloned.1.call-start = ((), (), s32[]{:S(2)}) async-start(), calls=%async_computation.4 | async-start | bytes 6266880 | tf_op jit(solution)/shard_map/reduce_scatter | solution.py:588
  415.8 1.6 copy-start.20
  415.8 1.6 copy-start.21
  417.3 1.9 collective-permute-start.8
  417.5 2.3 collective-permute-start.7
  423.7 1.2 copy-start.11
  423.8 203.2 %all-reduce.5.cloned.1.call-start = ((), (), s32[]{:S(2)}) async-start(), calls=%async_computation.6 | async-start | bytes 7520256 | tf_op jit(solution)/shard_map/psum | solution.py:591
  424.9 4.7 copy-start.7
  424.9 4.7 copy-start.8
  428.2 4.7 collective-permute-start.13
  432.8 5.3 copy-start.12
  432.8 2.6 collective-permute-start.12
  522.1 0.9 copy-start.16
  522.1 1.0 copy-start.19
  522.1 1.2 copy-start.6
  522.1 1.3 copy-start.18
  522.1 1.8 copy-start.24
  522.1 1.8 copy-start.25
  523.2 67.8 %collective-permute-start.6 = (bf16[96,1088]{1,0:T(8,128)(2,1)S(1)}, bf16[96,1088]{1,0:T(8,128)(2,1)S(1)}, u32[]{:S(2)}, u32[]{:S(2)}) collective-permute-start(bf16[96,1088]{1,0:T(8,128)(2,1)S(1)} %broadcast_select_fusion.19), channel_id=1, source_target_pairs={{0,64},{64,0},{1,65},{65,1},{2,66},{66,2},{3,67},{67,3},{4,68},{68... | collective-permute-start | bytes 626696 | tf_op jit(solution)/shard_map/ppermute | solution.py:504
  523.4 67.7 %collective-permute-start.5 = (bf16[96,1088]{1,0:T(8,128)(2,1)S(1)}, bf16[96,1088]{1,0:T(8,128)(2,1)S(1)}, u32[]{:S(2)}, u32[]{:S(2)}) collective-permute-start(bf16[96,1088]{1,0:T(8,128)(2,1)S(1)} %broadcast_select_fusion.21), channel_id=1, source_target_pairs={{0,64},{64,0},{1,65},{65,1},{2,66},{66,2},{3,67},{67,3},{4,68},{68... | collective-permute-start | bytes 626696 | tf_op jit(solution)/shard_map/ppermute | solution.py:504
  627.0 2.1 copy-start.3
  628.6 5.8 collective-permute-start.11
  629.0 4.5 copy-start.17
  629.1 5.3 copy-start.5
  630.8 3.6 copy-start.4
  630.8 11.8 %collective-permute-start.16 = (bf16[1088,1088]{1,0:T(8,128)(2,1)}, bf16[1088,1088]{1,0:T(8,128)(2,1)}, u32[]{:S(2)}, u32[]{:S(2)}) collective-permute-start(bf16[1088,1088]{1,0:T(8,128)(2,1)} %broadcast_select_fusion), channel_id=1, source_target_pairs={{0,64},{64,0},{1,65},{65,1},{2,66},{66,2},{3,67},{67,3},{4,68},{68... | collective-permute-start | bytes 7102472 | tf_op jit(solution)/shard_map/ppermute | solution.py:504
  642.6 7.1 %copy-start.1 = (bf16[2,96,1088]{2,1,0:T(8,128)(2,1)S(1)}, bf16[2,96,1088]{2,1,0:T(8,128)(2,1)}, u32[]{:S(2)}) copy-start(bf16[2,96,1088]{2,1,0:T(8,128)(2,1)} %param.8) | copy-start | bytes 1253380
Sparse Core Ops, SparseCore 0:
  14.5 57.4 all-gather.4
  74.3 55.5 all-gather.6
  306.9 55.1 reduce-scatter.4
  366.1 100.2 all-reduce.6
  469.4 52.6 reduce-scatter.2
  526.5 100.4 all-reduce.4

commit v2 on v1

v2 whole, which is shorter than its diff:
```python
import functools
import jax
import jax.numpy as jnp
from jax import lax
from jax.experimental import pallas as pl
from jax.experimental.pallas import tpu as pltpu
from jax.sharding import PartitionSpec as P

HEAD_DIM = 64
LOW = jnp.bfloat16
F32 = jnp.float32
MESH = pl.DeviceIdType.MESH


def dot_nn(left, right):
    return lax.dot_general(left, right, (((1,), (0,)), ((), ())), preferred_element_type=F32)


def dot_nt(left, right):
    return lax.dot_general(left, right, (((1,), (1,)), ((), ())), preferred_element_type=F32)


def dot_tn(left, right):
    return lax.dot_general(left, right, (((0,), (0,)), ((), ())), preferred_element_type=F32)


class Ring:
    def __init__(self, axis):
        whole = lax.axis_index("dp")
        rest = None
        if axis == "x":
            self.me = lax.axis_index("tensor")
        elif axis == "y":
            self.me, rest = lax.rem(whole, 4), lax.div(whole, 4) * 4
        else:
            self.me, rest = lax.div(whole, 4), lax.rem(whole, 4)
        self.right = lax.rem(self.me + 1, 4)
        self.left = lax.rem(self.me + 3, 4)
        self.opposite = lax.rem(self.me + 2, 4)

        def device(place):
            if axis == "x":
                return {"tensor": place}
            if axis == "y":
                return {"dp": rest + place}
            return {"dp": place * 4 + rest}

        self.to_right, self.to_left = device(self.right), device(self.left)


def sibling():
    return {"section": 1 - lax.axis_index("section")}


def greet(*targets):
    barrier = pltpu.get_barrier_semaphore()
    for target in targets:
        pl.semaphore_signal(barrier, inc=1, device_id=target, device_id_type=MESH)
    pl.semaphore_wait(barrier, len(targets))


def remote(src, dst, sems, which, target):
    return pltpu.make_async_remote_copy(
        src_ref=src,
        dst_ref=dst,
        send_sem=sems[0].at[which],
        recv_sem=sems[1].at[which],
        device_id=target,
        device_id_type=MESH,
    )


class Gather:
    def __init__(self, ring, slot, sems, own=None):
        self.ring, self.slot, self.sems = ring, slot, sems
        self.own = own if own is not None else lambda half: slot(ring.me, half)

    def copy(self, which, arriving=False):
        ring = self.ring
        half = (0, 1, 1, 0, 0, 1)[which]
        goes_right = which in (0, 2, 4)
        target = ring.to_right if goes_right else ring.to_left
        if which < 4:
            source_block = ring.left if goes_right else ring.right
            if not arriving:
                return remote(self.own(half), self.slot(ring.me, half), self.sems, which, target)
        else:
            source_block = ring.opposite
            if not arriving:
                handed = self.slot(ring.left if goes_right else ring.right, half)
                return remote(handed, handed, self.sems, which, target)
        part = self.slot(source_block, half)
        return remote(part, part, self.sems, which, target)

    def start(self):
        for which in range(4):
            self.copy(which).start()

    def relay(self):
        for which in (0, 1):
            self.copy(which, arriving=True).wait_recv()
            self.copy(which + 4).start()

    def wait_left(self):
        self.copy(2, arriving=True).wait_recv()

    def wait_right(self):
        self.copy(3, arriving=True).wait_recv()

    def wait_opposite(self):
        self.copy(4, arriving=True).wait_recv()
        self.copy(5, arriving=True).wait_recv()

    def wait_all(self):
        self.wait_left()
        self.wait_right()
        self.wait_opposite()

    def finish(self):
        for which in range(6):
            self.copy(which).wait_send()


class Scatter:
    def __init__(self, ring, part, landing, passing, arrived, sems):
        self.ring, self.part, self.landing, self.passing = ring, part, landing, passing
        self.arrived, self.sems = arrived, sems

    def copy(self, which):
        ring = self.ring
        half = (0, 1, 1, 0, 0, 1)[which]
        goes_right = which in (0, 2, 4)
        if which < 2:
            src, dst = self.part(ring.opposite, half), self.landing(half)
        else:
            dst = self.arrived(0 if goes_right else 1, half)
            if which < 4:
                src = self.part(ring.right if goes_right else ring.left, half)
            else:
                src = self.passing(half)
        return remote(src, dst, self.sems, which, ring.to_right if goes_right else ring.to_left)

    def start_near(self):
        self.copy(2).start()
        self.copy(3).start()

    def start_far(self):
        self.copy(0).start()
        self.copy(1).start()

    def relay(self):
        for half, block in ((0, self.ring.right), (1, self.ring.left)):
            self.copy(half).wait_recv()
            added = self.part(block, half)[...].astype(F32) + self.landing(half)[...].astype(F32)
            self.passing(half)[...] = added.astype(LOW)
            self.copy(half + 4).start()

    def wait(self):
        for which in (2, 3, 4, 5):
            self.copy(which).wait_recv()

    def total(self, half):
        return (
            self.part(self.ring.me, half)[...].astype(F32)
            + self.arrived(0, half)[...].astype(F32)
            + self.arrived(1, half)[...].astype(F32)
        )

    def finish(self):
        for which in range(6):
            self.copy(which).wait_send()


def row_gather(ring, full, sems):
    half = full.shape[1] // 2
    return Gather(ring, lambda block, which: full.at[block, pl.ds(which * half, half)], sems)


def row_scatter(ring, parts, landing, passing, arrived, sems):
    half = parts.shape[1] // 2

    def rows(which):
        return pl.ds(which * half, half)

    return Scatter(
        ring,
        lambda block, which: parts.at[block, rows(which)],
        lambda which: landing.at[which],
        lambda which: passing.at[which],
        lambda side, which: arrived.at[side, rows(which)],
        sems,
    )


def row_total(scatter):
    scatter.wait()
    return jnp.concatenate([scatter.total(0), scatter.total(1)], axis=0)


def norm_stats(values):
    average = jnp.mean(values, axis=-1, keepdims=True)
    centered = values - average
    variance = jnp.mean(centered * centered, axis=-1, keepdims=True)
    scale = lax.rsqrt(variance + 1e-05)
    return centered * scale, scale


def norm_back(values, gain, grad):
    xhat, scale = norm_stats(values)
    scaled = grad * gain
    part = scale * (
        scaled
        - jnp.mean(scaled, axis=-1, keepdims=True)
        - xhat * jnp.mean(scaled * xhat, axis=-1, keepdims=True)
    )
    return part, jnp.sum(grad * xhat, axis=0, keepdims=True)


def gelu_tanh(values):
    inner = 0.7978845608028654 * (values + 0.044715 * values * values * values)
    return 0.5 * values * (1.0 + jnp.tanh(inner))


def gelu_slope(values):
    square = values * values
    bent = jnp.tanh(0.7978845608028654 * values * (1.0 + 0.044715 * square))
    slope = 0.7978845608028654 * (1.0 + 3.0 * 0.044715 * square)
    return 0.5 * (1.0 + bent) + 0.5 * values * (1.0 - bent * bent) * slope


def pick_copies(layer, mine, theirs, target, sem):
    def start():
        mine_here = lax.axis_index("section") == layer

        @pl.when(mine_here)
        def _():
            pltpu.make_async_copy(mine, target, sem).start()

        @pl.when(jnp.logical_not(mine_here))
        def _():
            pltpu.make_async_copy(theirs, target, sem).start()

    def wait():
        pltpu.make_async_copy(mine, target, sem).wait()

    return start, wait


def pair_columns(features):
    width = 2 * HEAD_DIM
    return [
        (start, min(width, features - start)) for start in range(0, features, width)
    ]


def head_masks(width):
    lanes = lax.broadcasted_iota(jnp.int32, (1, width), 1)
    if width == HEAD_DIM:
        return [None]
    return [lanes < HEAD_DIM, lanes >= HEAD_DIM]


def masked(values, mask):
    return values if mask is None else jnp.where(mask, values, jnp.zeros_like(values))


def attention_weights(layer, mine, theirs, target, sems):
    return [
        pick_copies(layer, mine.at[which], theirs.at[which], target.at[which], sems.at[which])
        for which in range(4)
    ]


def forward_kernel(
    layer, features, x_ref, bias_ref, gains_ref, at_mine, at_theirs, up_mine, up_theirs, down_mine,
    down_theirs, y_ref, middle_ref, one_ref, query_ref, key_ref, value_ref, mixed_ref, two_ref,
    act_ref, hidden_ref, at_w, up_w, down_w, weight_sems, parts, landing, passing, arrived,
    key_send, key_recv, value_send, value_recv, two_send, two_recv, sum_send, sum_recv,
):
    ring = Ring("x")
    me = ring.me
    fetches = attention_weights(layer, at_mine, at_theirs, at_w, weight_sems)
    fetches.append(pick_copies(layer, up_mine, up_theirs, up_w, weight_sems.at[4]))
    fetches.append(pick_copies(layer, down_mine, down_theirs, down_w, weight_sems.at[5]))
    for which in (1, 2, 0, 3, 4, 5):
        fetches[which][0]()
    greet(ring.to_right, ring.to_left)
    rows = x_ref.shape[0]
    inputs = x_ref[...].astype(F32)
    xhat, _ = norm_stats(inputs)
    one_ref[...] = (xhat * gains_ref[0:1, :]).astype(LOW)
    normed_one = one_ref[...]
    fetches[1][1]()
    key_ref[me] = dot_nn(normed_one, at_w[1]).astype(LOW)
    keys = row_gather(ring, key_ref, (key_send, key_recv))
    keys.start()
    fetches[2][1]()
    value_ref[me] = dot_nn(normed_one, at_w[2]).astype(LOW)
    values = row_gather(ring, value_ref, (value_send, value_recv))
    values.start()
    fetches[0][1]()
    query_ref[...] = dot_nn(normed_one, at_w[0]).astype(LOW)
    keys.relay()
    values.relay()
    keys.wait_all()
    values.wait_all()
    fetches[3][1]()
    bias = bias_ref[...]
    for begin, width in pair_columns(features):
        columns = pl.ds(begin, width)
        queries = query_ref[:, columns]
        key_block = key_ref[:, :, columns].reshape(4 * rows, width)
        value_block = value_ref[:, :, columns].reshape(4 * rows, width)
        mixed = None
        for mask in head_masks(width):
            scores = dot_nt(masked(queries, mask), key_block) * 0.125 + bias
            raised = jnp.exp(scores - jnp.max(scores, axis=-1, keepdims=True))
            probs = raised * (1.0 / jnp.sum(raised, axis=-1, keepdims=True))
            own = dot_nn(probs.astype(LOW), value_block)
            mixed = own if mixed is None else jnp.where(mask, own, mixed)
        mixed_ref[:, columns] = mixed.astype(LOW)
    middle_ref[...] = x_ref[...].astype(F32) + dot_nn(mixed_ref[...], at_w[3])
    xhat, _ = norm_stats(middle_ref[...])
    two_ref[me] = (xhat * gains_ref[1:2, :]).astype(LOW)
    tokens = row_gather(ring, two_ref, (two_send, two_recv))
    tokens.start()
    fetches[4][1]()
    fetches[5][1]()
    sums = row_scatter(ring, parts, landing, passing, arrived, (sum_send, sum_recv))

    def feed(block):
        act_ref[block] = dot_nn(two_ref[block], up_w[...])
        hidden_ref[block] = gelu_tanh(act_ref[block]).astype(LOW)
        parts[block] = dot_nn(hidden_ref[block], down_w[...]).astype(LOW)

    feed(me)
    tokens.relay()
    tokens.wait_left()
    feed(ring.left)
    tokens.wait_right()
    feed(ring.right)
    sums.start_near()
    tokens.wait_opposite()
    feed(ring.opposite)
    sums.start_far()
    sums.relay()
    y_ref[...] = (middle_ref[...] + row_total(sums)).astype(LOW)
    keys.finish()
    values.finish()
    tokens.finish()
    sums.finish()


def scatter_scratch(rows, features):
    return [
        pltpu.VMEM((4, rows, features), LOW),
        pltpu.VMEM((2, rows // 2, features), LOW),
        pltpu.VMEM((2, rows // 2, features), LOW),
        pltpu.VMEM((2, rows, features), LOW),
    ]


def weight_scratch(features, hidden):
    return [
        pltpu.VMEM((4, features, features), LOW),
        pltpu.VMEM((features, hidden), LOW),
        pltpu.VMEM((hidden, features), LOW),
        pltpu.SemaphoreType.DMA((6,)),
    ]


def in_vmem():
    return pl.BlockSpec(memory_space=pltpu.VMEM)


def anywhere():
    return pl.BlockSpec(memory_space=pl.ANY)


def forward_layer(layer, x, bias, gains, attention, feed):
    rows, features = x.shape
    hidden = feed[0].shape[1]
    out_shape = (
        jax.ShapeDtypeStruct((rows, features), LOW),
        jax.ShapeDtypeStruct((rows, features), F32),
        jax.ShapeDtypeStruct((rows, features), LOW),
        jax.ShapeDtypeStruct((rows, features), LOW),
        jax.ShapeDtypeStruct((4, rows, features), LOW),
        jax.ShapeDtypeStruct((4, rows, features), LOW),
        jax.ShapeDtypeStruct((rows, features), LOW),
        jax.ShapeDtypeStruct((4, rows, features), LOW),
        jax.ShapeDtypeStruct((4, rows, hidden), F32),
        jax.ShapeDtypeStruct((4, rows, hidden), LOW),
    )
    return pl.pallas_call(
        functools.partial(forward_kernel, layer, features),
        out_shape=out_shape,
        in_specs=[in_vmem()] * 3 + [anywhere()] * 6,
        out_specs=[in_vmem()] * len(out_shape),
        scratch_shapes=weight_scratch(features, hidden)
        + scatter_scratch(rows, features)
        + [pltpu.SemaphoreType.DMA((6,))] * 8,
        compiler_params=pltpu.CompilerParams(
            collective_id=layer, has_side_effects=True, vmem_limit_bytes=56 * 2**20
        ),
        cost_estimate=pl.CostEstimate(
            flops=3 * 10**9, bytes_accessed=24 * 10**6, transcendentals=10**6
        ),
        name=f"layer_forward_{layer}",
    )(x, bias, gains, *attention, *feed)


def backward_kernel(
    layer, features, x_ref, dy_ref, bias_ref, gains_ref, middle_ref, query_ref, key_ref, value_ref,
    act_ref, at_mine, at_theirs, up_mine, up_theirs, down_mine, down_theirs,
    dx_ref, gain_ref, out_ref, pre_ref, branch_ref, dquery_ref, dkey_ref, dvalue_ref,
    at_w, up_w, down_w, weight_sems, parts, landing, passing, arrived, parts_b, landing_b,
    passing_b, arrived_b, parts_c, landing_c, passing_c, arrived_c, mixed_grad,
    out_send, out_recv, sum_send, sum_recv, key_send, key_recv, value_send, value_recv,
):
    ring = Ring("x")
    me = ring.me
    fetches = attention_weights(layer, at_mine, at_theirs, at_w, weight_sems)
    fetches.append(pick_copies(layer, up_mine, up_theirs, up_w, weight_sems.at[4]))
    fetches.append(pick_copies(layer, down_mine, down_theirs, down_w, weight_sems.at[5]))
    for which in (5, 4, 3, 0, 1, 2):
        fetches[which][0]()
    rows = x_ref.shape[0]
    out_ref[me] = dy_ref[...]
    greet(ring.to_right, ring.to_left)
    grads = row_gather(ring, out_ref, (out_send, out_recv))
    grads.start()
    sums = row_scatter(ring, parts, landing, passing, arrived, (sum_send, sum_recv))
    fetches[5][1]()
    fetches[4][1]()

    def feed(block):
        hidden_grad = dot_nt(out_ref[block], down_w[...])
        pre_ref[block] = (hidden_grad * gelu_slope(act_ref[block])).astype(LOW)
        parts[block] = dot_nt(pre_ref[block], up_w[...]).astype(LOW)

    feed(me)
    grads.relay()
    grads.wait_left()
    feed(ring.left)
    grads.wait_right()
    feed(ring.right)
    sums.start_near()
    grads.wait_opposite()
    feed(ring.opposite)
    sums.start_far()
    sums.relay()
    middle_part, gain_two = norm_back(middle_ref[...], gains_ref[1:2, :], row_total(sums))
    gain_ref[1:2, :] = gain_two
    middle_grad = dy_ref[...].astype(F32) + middle_part
    middle_ref_grad = middle_grad
    branch_ref[...] = middle_grad.astype(LOW)
    fetches[3][1]()
    mixed_grad[...] = dot_nt(branch_ref[...], at_w[3]).astype(LOW)
    bias = bias_ref[...]
    for begin, width in pair_columns(features):
        columns = pl.ds(begin, width)
        queries = query_ref[:, columns]
        outer = mixed_grad[:, columns]
        key_block = key_ref[:, :, columns].reshape(4 * rows, width)
        value_block = value_ref[:, :, columns].reshape(4 * rows, width)
        dquery = dkey = dvalue = None
        for mask in head_masks(width):
            query_one, outer_one = masked(queries, mask), masked(outer, mask)
            scores = dot_nt(key_block, query_one) * 0.125 + bias
            raised = jnp.exp(scores - jnp.max(scores, axis=0, keepdims=True))
            probs = raised * (1.0 / jnp.sum(raised, axis=0, keepdims=True))
            probs_grad = dot_nt(value_block, outer_one)
            mean = jnp.sum(probs * probs_grad, axis=0, keepdims=True)
            score_grad = (probs * (probs_grad - mean)).astype(LOW)
            own_query = dot_tn(score_grad, key_block)
            own_key = dot_nn(score_grad, query_one)
            own_value = dot_nn(probs.astype(LOW), outer_one)
            if dquery is None:
                dquery, dkey, dvalue = own_query, own_key, own_value
            else:
                dquery = jnp.where(mask, own_query, dquery)
                dkey, dvalue = dkey + own_key, dvalue + own_value
        dquery_ref[:, columns] = (dquery * 0.125).astype(LOW)
        parts_b[:, :, columns] = (dkey * 0.125).astype(LOW).reshape(4, rows, width)
        parts_c[:, :, columns] = dvalue.astype(LOW).reshape(4, rows, width)
    dkeys = row_scatter(ring, parts_b, landing_b, passing_b, arrived_b, (key_send, key_recv))
    dvalues = row_scatter(
        ring, parts_c, landing_c, passing_c, arrived_c, (value_send, value_recv)
    )
    dkeys.start_far()
    dvalues.start_far()
    dkeys.start_near()
    dvalues.start_near()
    for which in (0, 1, 2):
        fetches[which][1]()
    one_grad = dot_nt(dquery_ref[...], at_w[0])
    dkeys.relay()
    dvalues.relay()
    dkey_ref[...] = row_total(dkeys).astype(LOW)
    dvalue_ref[...] = row_total(dvalues).astype(LOW)
    one_grad = one_grad + dot_nt(dkey_ref[...], at_w[1]) + dot_nt(dvalue_ref[...], at_w[2])
    inputs_part, gain_one = norm_back(x_ref[...].astype(F32), gains_ref[0:1, :], one_grad)
    gain_ref[0:1, :] = gain_one
    dx_ref[...] = (middle_ref_grad + inputs_part).astype(LOW)
    grads.finish()
    sums.finish()
    dkeys.finish()
    dvalues.finish()


def backward_layer(layer, x, dy, bias, gains, middle, query, key, value, act, attention, feed):
    rows, features = x.shape
    hidden = feed[0].shape[1]
    out_shape = (
        jax.ShapeDtypeStruct((rows, features), LOW),
        jax.ShapeDtypeStruct((2, features), F32),
        jax.ShapeDtypeStruct((4, rows, features), LOW),
        jax.ShapeDtypeStruct((4, rows, hidden), LOW),
        jax.ShapeDtypeStruct((rows, features), LOW),
        jax.ShapeDtypeStruct((rows, features), LOW),
        jax.ShapeDtypeStruct((rows, features), LOW),
        jax.ShapeDtypeStruct((rows, features), LOW),
    )
    return pl.pallas_call(
        functools.partial(backward_kernel, layer, features),
        out_shape=out_shape,
        in_specs=[in_vmem()] * 9 + [anywhere()] * 6,
        out_specs=[in_vmem()] * len(out_shape),
        scratch_shapes=weight_scratch(features, hidden)
        + scatter_scratch(rows, features) * 3
        + [pltpu.VMEM((rows, features), LOW)]
        + [pltpu.SemaphoreType.DMA((6,))] * 8,
        compiler_params=pltpu.CompilerParams(
            collective_id=2 + layer, has_side_effects=True, vmem_limit_bytes=56 * 2**20
        ),
        cost_estimate=pl.CostEstimate(
            flops=4 * 10**9, bytes_accessed=24 * 10**6, transcendentals=10**6
        ),
        name=f"layer_backward_{layer}",
    )(x, dy, bias, gains, middle, query, key, value, act, *attention, *feed)


X_ROWS, Y_ROWS = 48, 112


def weights_kernel(
    shard_ref, gain_ref, mine_ref, theirs_ref, gain_mine, gain_theirs, local_sems, x_send, x_recv,
    yx_send, yx_recv, zx_send, zx_recv, y_send, y_recv, z_send, z_recv, gain_send, gain_recv,
    pair_send, pair_recv,
):
    x_ring, y_ring, z_ring = Ring("x"), Ring("y"), Ring("z")
    mine_y, mine_z, mine_x = y_ring.me, z_ring.me, x_ring.me
    share = shard_ref.shape[1]
    y_begin, z_begin = X_ROWS, X_ROWS + Y_ROWS
    z_rows = share - z_begin
    all_x, all_y, all_z = pl.ds(0, X_ROWS), pl.ds(y_begin, Y_ROWS), pl.ds(z_begin, z_rows)
    y_half = (pl.ds(y_begin, 64), pl.ds(y_begin + 64, Y_ROWS - 64))
    z_half = (pl.ds(z_begin, 64), pl.ds(z_begin + 64, z_rows - 64))
    pair = sibling()
    greet(
        x_ring.to_right, x_ring.to_left, y_ring.to_right, y_ring.to_left, z_ring.to_right,
        z_ring.to_left, pair,
    )
    locals_ = [
        pltpu.make_async_copy(
            shard_ref.at[mine_y, all_y], mine_ref.at[mine_y, mine_x, all_y], local_sems.at[0]
        ),
        pltpu.make_async_copy(
            shard_ref.at[mine_z, all_z], mine_ref.at[mine_z, mine_x, all_z], local_sems.at[1]
        ),
        pltpu.make_async_copy(
            shard_ref.at[:, all_x], mine_ref.at[:, mine_x, all_x], local_sems.at[2]
        ),
        pltpu.make_async_copy(gain_ref, gain_mine.at[mine_x], local_sems.at[3]),
    ]
    first_y = Gather(
        x_ring,
        lambda block, half: mine_ref.at[mine_y, block, y_half[half]],
        (yx_send, yx_recv),
        lambda half: shard_ref.at[mine_y, y_half[half]],
    )
    first_z = Gather(
        x_ring,
        lambda block, half: mine_ref.at[mine_z, block, z_half[half]],
        (zx_send, zx_recv),
        lambda half: shard_ref.at[mine_z, z_half[half]],
    )
    along_x = Gather(
        x_ring,
        lambda block, half: mine_ref.at[pl.ds(2 * half, 2), block, all_x],
        (x_send, x_recv),
        lambda half: shard_ref.at[pl.ds(2 * half, 2), all_x],
    )
    along_y = Gather(
        y_ring,
        lambda block, half: mine_ref.at[block, pl.ds(2 * half, 2), all_y],
        (y_send, y_recv),
    )
    along_z = Gather(
        z_ring,
        lambda block, half: mine_ref.at[block, pl.ds(2 * half, 2), all_z],
        (z_send, z_recv),
    )

    def gain_copy(which, block, src=None):
        part = gain_mine.at[block]
        target = x_ring.to_left if which == 1 else x_ring.to_right
        return remote(part if src is None else src, part, (gain_send, gain_recv), which, target)

    def hand(which, region):
        return remote(mine_ref.at[region], theirs_ref.at[region], (pair_send, pair_recv), which, pair)

    handed = []

    def hand_on(which, region):
        copy = hand(which, region)
        copy.start()
        handed.append(copy)

    first_y.start()
    first_z.start()
    for copy in locals_:
        copy.start()
    gain_copy(0, mine_x, gain_ref).start()
    gain_copy(1, mine_x, gain_ref).start()
    along_x.start()
    first_y.relay()
    first_z.relay()
    first_y.wait_all()
    locals_[0].wait()
    along_y.start()
    hand_on(0, (mine_y, slice(None), all_y))
    first_z.wait_all()
    locals_[1].wait()
    along_z.start()
    hand_on(1, (mine_z, slice(None), all_z))
    gain_copy(0, x_ring.left).wait_recv()
    gain_copy(2, x_ring.left).start()
    along_x.relay()
    along_y.relay()
    along_z.relay()
    along_x.wait_all()
    locals_[2].wait()
    hand_on(2, (slice(None), slice(None), all_x))
    along_y.wait_left()
    hand_on(3, (y_ring.left, slice(None), all_y))
    along_z.wait_left()
    hand_on(4, (z_ring.left, slice(None), all_z))
    along_y.wait_right()
    hand_on(5, (y_ring.right, slice(None), all_y))
    along_z.wait_right()
    hand_on(6, (z_ring.right, slice(None), all_z))
    gain_copy(1, x_ring.right).wait_recv()
    gain_copy(2, x_ring.opposite).wait_recv()
    locals_[3].wait()
    gains = remote(gain_mine, gain_theirs, (pair_send, pair_recv), 9, pair)
    gains.start()
    along_y.wait_opposite()
    hand_on(7, (y_ring.opposite, slice(None), all_y))
    along_z.wait_opposite()
    hand_on(8, (z_ring.opposite, slice(None), all_z))
    for copy in handed + [gains]:
        copy.wait()
    for which in range(3):
        gain_copy(which, mine_x).wait_send()
    for gather in (first_y, first_z, along_x, along_y, along_z):
        gather.finish()


def gather_weights(shard, gain):
    mats, share, features = shard.shape
    full = jax.ShapeDtypeStruct((mats, 4, share, features), LOW)
    gains = jax.ShapeDtypeStruct((4,) + gain.shape, LOW)
    return pl.pallas_call(
        weights_kernel,
        out_shape=(full, full, gains, gains),
        in_specs=[anywhere()] * 2,
        out_specs=[anywhere()] * 4,
        scratch_shapes=[pltpu.SemaphoreType.DMA((4,))]
        + [pltpu.SemaphoreType.DMA((6,))] * 10
        + [pltpu.SemaphoreType.DMA((3,))] * 2
        + [pltpu.SemaphoreType.DMA((10,))] * 2,
        compiler_params=pltpu.CompilerParams(collective_id=4, has_side_effects=True),
        cost_estimate=pl.CostEstimate(flops=0, bytes_accessed=60 * 10**6, transcendentals=0),
        name="gather_weights",
    )(shard, gain)


class SmallSum:
    def __init__(self, ring, slots, sems):
        self.ring, self.slots, self.sems = ring, slots, sems

    def copy(self, which, block):
        target = self.ring.to_left if which == 1 else self.ring.to_right
        part = self.slots.at[block]
        return remote(part, part, self.sems, which, target)

    def start(self):
        self.copy(0, self.ring.me).start()
        self.copy(1, self.ring.me).start()

    def relay(self):
        self.copy(0, self.ring.left).wait_recv()
        self.copy(2, self.ring.left).start()

    def result(self):
        self.copy(1, self.ring.right).wait_recv()
        self.copy(2, self.ring.opposite).wait_recv()
        return (self.slots[0] + self.slots[1]) + (self.slots[2] + self.slots[3])

    def finish(self):
        for which in range(3):
            self.copy(which, self.ring.me).wait_send()


def gradient_kernel(features, *refs):
    (two_a, two_b, pre_a, pre_b, hid_a, hid_b, out_a, out_b, one_a, one_b, mix_a, mix_b, dq_a, dq_b,
     dk_a, dk_b, dv_a, dv_b, br_a, br_b, y_a, y_b, dx_a, dx_b, gain_in,
     feed_out, feed_other, at_out, at_other, act_out, grad_out, gain_out,
     feed_in, at_left, at_right, at_sum, feed_sum,
     xl, xp, xa, fl, fp, fa, fs, fr, al, ap, aa, as_, ar, ad, gain_pair, gain_x, gain_y, gain_z,
     local_sems, swap_send, swap_recv, x_send, x_recv, f_send, f_recv, fg_send, fg_recv, fh_send,
     fh_recv, a_send, a_recv, ag_send, ag_recv, ah_send, ah_recv, gain_send, gain_recv, end_send,
     end_recv, keep_sems) = refs
    x_ring, y_ring, z_ring = Ring("x"), Ring("y"), Ring("z")
    pair = sibling()
    section = lax.axis_index("section")
    share = features // 4
    greet(
        x_ring.to_right, x_ring.to_left, y_ring.to_right, y_ring.to_left, z_ring.to_right,
        z_ring.to_left, pair,
    )
    layers = (
        (two_a, pre_a, hid_a, out_a, one_a, mix_a, dq_a, dk_a, dv_a, br_a, y_a, dx_a),
        (two_b, pre_b, hid_b, out_b, one_b, mix_b, dq_b, dk_b, dv_b, br_b, y_b, dx_b),
    )

    def both(layer, first):
        (two, pre, hidden, out, one, mixed, dq, dk, dv, branch, _, _) = layers[layer]
        zero = (one, one, dq, dk, two, pre)
        other = (one, mixed, dv, branch, hidden, out)
        own, sent = (zero, other) if first else (other, zero)
        targets = [
            at_left.at[layer, 0], at_left.at[layer, 1], at_right.at[layer, 0],
            at_right.at[layer, 1], feed_in.at[layer, 0], feed_in.at[layer, 1],
        ]
        keeps = [
            pltpu.make_async_copy(ref, target.at[0], local_sems.at[layer * 6 + which])
            for which, (ref, target) in enumerate(zip(own, targets))
        ]
        sends = [
            remote(ref, target.at[1], (swap_send, swap_recv), layer * 6 + which, pair)
            for which, (ref, target) in enumerate(zip(sent, targets))
        ]
        return keeps, sends

    def start_inputs(first):
        for which in range(6):
            for layer in (1, 0):
                for copy in both(layer, first):
                    copy[which].start()

    def last_copies(layer):
        _, _, _, _, _, _, _, _, _, _, y, dx = layers[layer]
        return (
            remote(y, act_out.at[section], (swap_send, swap_recv), 12, pair),
            remote(dx, grad_out.at[section], (swap_send, swap_recv), 13, pair),
        )

    def keep_copies(layer):
        _, _, _, _, _, _, _, _, _, _, y, dx = layers[layer]
        return (
            pltpu.make_async_copy(y, act_out.at[section], keep_sems.at[0]),
            pltpu.make_async_copy(dx, grad_out.at[section], keep_sems.at[1]),
        )

    @pl.when(section == 0)
    def _():
        start_inputs(True)
        for copy in last_copies(1) + keep_copies(0):
            copy.start()

    @pl.when(section == 1)
    def _():
        start_inputs(False)
        for copy in last_copies(0) + keep_copies(1):
            copy.start()

    gain_pair[0] = gain_in[...]
    swap_gain = remote(gain_pair.at[0], gain_pair.at[1], (gain_send, gain_recv), 9, pair)
    swap_gain.start()

    def wait_inputs(layer, whiches):
        keeps, sends = both(layer, True)
        for which in whiches:
            keeps[which].wait()
            sends[which].wait_recv()

    x_sums, f_sums, f_mids, f_ends, a_sums, a_mids, a_ends = [], [], [], [], [], [], []
    f_half = ((0, 144), (144, share - 144))
    a_half = ((0, 80), (80, 64))
    for layer in range(2):

        def x_part(block, half, layer=layer):
            return at_sum.at[layer, half, pl.ds(pl.multiple_of(block * share, 16), share)]

        def pick(ref, layer=layer):
            return lambda half: ref.at[layer, half]

        def pick_side(ref, halves, layer=layer):
            return lambda side, half: ref.at[layer, side, pl.ds(*halves[half])]

        def pick_half(ref, halves, layer=layer):
            return lambda half: ref.at[layer, pl.ds(*halves[half])]

        def pick_slot(ref, halves, layer=layer):
            return lambda block, half: ref.at[layer, block, pl.ds(*halves[half])]

        def sems(send, recv, layer=layer):
            return send.at[layer], recv.at[layer]

        def f_part(block, half, layer=layer):
            begin, size = f_half[half]
            return feed_sum.at[layer, pl.ds(pl.multiple_of(block * share + begin, 16), size)]

        def a_part(block, half, layer=layer):
            begin, size = a_half[half]
            row = lax.rem(block, 2) * 144 + begin
            return ad.at[layer, lax.div(block, 2), pl.ds(pl.multiple_of(row, 16), size)]

        def a_out(block, half, layer=layer):
            begin, size = a_half[half]
            row = lax.rem(block, 2) * 144 + begin
            return at_out.at[layer, lax.div(block, 2), pl.ds(pl.multiple_of(row, 16), size)]

        x_sums.append(
            Scatter(
                x_ring, x_part, pick(xl), pick(xp),
                lambda side, half, layer=layer: xa.at[layer, side, half], sems(x_send, x_recv),
            )
        )
        near, far = (y_ring, z_ring) if layer == 0 else (z_ring, y_ring)
        f_sums.append(
            Scatter(
                near, f_part, pick_half(fl, f_half), pick_half(fp, f_half),
                pick_side(fa, f_half), sems(f_send, f_recv),
            )
        )
        f_mids.append(Gather(far, pick_slot(fs, f_half), sems(fg_send, fg_recv)))
        f_ends.append(
            Gather(near, pick_slot(feed_out, f_half), sems(fh_send, fh_recv), pick_half(fr, f_half))
        )
        a_sums.append(
            Scatter(
                near, a_part, pick_half(al, a_half), pick_half(ap, a_half),
                pick_side(aa, a_half), sems(a_send, a_recv),
            )
        )
        a_mids.append(Gather(far, pick_slot(as_, a_half), sems(ag_send, ag_recv)))
        a_ends.append(Gather(near, a_out, sems(ah_send, ah_recv), pick_half(ar, a_half)))

    chunks = [(begin, min(256, features - begin)) for begin in range(0, features, 256)]

    def attention_products(layer):
        wait_inputs(layer, (0, 1, 2, 3))
        for which in range(2):
            right = at_right[layer, which].reshape(-1, features)
            for begin, size in chunks:
                left = at_left[layer, which, :, :, pl.ds(begin, size)].reshape(-1, size)
                at_sum[layer, which, pl.ds(begin, size)] = dot_tn(left, right).astype(LOW)
        x_sums[layer].start_far()
        x_sums[layer].start_near()

    def feed_products(layer):
        wait_inputs(layer, (4, 5))
        right = feed_in[layer, 1].reshape(-1, features)
        for begin, size in chunks:
            left = feed_in[layer, 0, :, :, :, pl.ds(begin, size)].reshape(-1, size)
            feed_sum[layer, pl.ds(begin, size)] = dot_tn(left, right).astype(LOW)
        f_sums[layer].start_far()
        f_sums[layer].start_near()

    def feed_middle(layer):
        f_sums[layer].wait()
        place = f_mids[layer].ring.me
        for half in range(2):
            fs[layer, place, pl.ds(*f_half[half])] = f_sums[layer].total(half).astype(LOW)
        f_mids[layer].start()

    def four(ref, layer, halves, half):
        rows = pl.ds(*halves[half])
        return (ref[layer, 0, rows].astype(F32) + ref[layer, 1, rows].astype(F32)) + (
            ref[layer, 2, rows].astype(F32) + ref[layer, 3, rows].astype(F32)
        )

    def feed_end(layer):
        f_mids[layer].wait_all()
        for half in range(2):
            fr[layer, pl.ds(*f_half[half])] = four(fs, layer, f_half, half).astype(LOW)
        f_ends[layer].start()
        pltpu.make_async_copy(
            fr.at[layer], feed_out.at[layer, f_ends[layer].ring.me], keep_sems.at[2 + layer]
        ).start()

    def attention_middle(layer):
        x_sums[layer].wait()
        for half in range(2):
            ad[layer, half, pl.ds(0, share)] = x_sums[layer].total(half).astype(LOW)
            ad[layer, half, pl.ds(share, 288 - share)] = jnp.zeros((288 - share, features), LOW)
        a_sums[layer].start_far()
        a_sums[layer].start_near()

    def attention_far(layer):
        a_sums[layer].wait()
        place = a_mids[layer].ring.me
        for half in range(2):
            as_[layer, place, pl.ds(*a_half[half])] = a_sums[layer].total(half).astype(LOW)
        a_mids[layer].start()

    def own_attention(layer):
        block = a_ends[layer].ring.me
        row = pl.multiple_of(lax.rem(block, 2) * 144, 16)
        return pltpu.make_async_copy(
            ar.at[layer], at_out.at[layer, lax.div(block, 2), pl.ds(row, 144)],
            keep_sems.at[4 + layer],
        )

    def attention_end(layer):
        a_mids[layer].wait_all()
        for half in range(2):
            ar[layer, pl.ds(*a_half[half])] = four(as_, layer, a_half, half).astype(LOW)
        a_ends[layer].start()
        own_attention(layer).start()

    attention_products(1)
    attention_products(0)
    feed_products(0)
    feed_products(1)

    swap_gain.wait()
    gain_x[x_ring.me] = gain_pair[0] + gain_pair[1]
    small = [
        SmallSum(ring, slots, (gain_send.at[pl.ds(3 * i, 3)], gain_recv.at[pl.ds(3 * i, 3)]))
        for i, (ring, slots) in enumerate(((x_ring, gain_x), (y_ring, gain_y), (z_ring, gain_z)))
    ]
    small[0].start()
    x_sums[1].relay()
    f_sums[0].relay()
    f_sums[1].relay()
    small[0].relay()
    feed_middle(0)
    feed_middle(1)
    gain_y[y_ring.me] = small[0].result()
    small[1].start()
    f_mids[0].relay()
    f_mids[1].relay()
    x_sums[0].relay()
    small[1].relay()
    attention_middle(1)
    feed_end(0)
    feed_end(1)
    gain_z[z_ring.me] = small[1].result()
    small[2].start()
    a_sums[1].relay()
    f_ends[0].relay()
    f_ends[1].relay()
    small[2].relay()
    attention_far(1)
    attention_middle(0)
    a_mids[1].relay()
    attention_end(1)
    a_sums[0].relay()
    a_ends[1].relay()
    gain_out[...] = small[2].result()

    for layer in range(2):
        f_ends[layer].wait_all()
        pltpu.make_async_copy(
            fr.at[layer], feed_out.at[layer, f_ends[layer].ring.me], keep_sems.at[2 + layer]
        ).wait()
    end_feed = remote(feed_out.at[1 - section], feed_other, (end_send, end_recv), 0, pair)
    end_feed.start()

    attention_far(0)
    a_mids[0].relay()
    attention_end(0)
    a_ends[0].relay()
    for layer in (1, 0):
        a_ends[layer].wait_all()
        own_attention(layer).wait()
    end_attention = remote(at_out.at[1 - section], at_other, (end_send, end_recv), 1, pair)
    end_attention.start()
    for layer in range(2):
        for copy in both(layer, True)[1]:
            copy.wait_send()
        for many in (x_sums, f_sums, f_mids, f_ends, a_sums, a_mids, a_ends):
            many[layer].finish()
    for each in small:
        each.finish()
    for copy in last_copies(0):
        copy.wait()
    for copy in keep_copies(0):
        copy.wait()
    end_feed.wait()
    end_attention.wait()


def sum_gradients(features, rows, operands, gain):
    share = features // 4
    dma = pltpu.SemaphoreType.DMA

    def low(*shape):
        return pltpu.VMEM(shape + (features,), LOW)

    def out(*shape):
        return jax.ShapeDtypeStruct(shape + (features,), LOW)

    return pl.pallas_call(
        functools.partial(gradient_kernel, features),
        out_shape=(
            out(2, 4, share), out(4, share), out(2, 2, 288), out(2, 288), out(2, rows),
            out(2, rows), jax.ShapeDtypeStruct((8, features), F32),
        ),
        in_specs=[anywhere()] * 24 + [in_vmem()],
        out_specs=[anywhere()] * 6 + [in_vmem()],
        scratch_shapes=[
            low(2, 2, 2, 4, rows), low(2, 2, 2, rows), low(2, 2, 2, rows),
            low(2, 2, features), low(2, features),
            low(2, 2, share), low(2, 2, share), low(2, 2, 2, share),
            low(2, share), low(2, share), low(2, 2, share), low(2, 4, share), low(2, share),
            low(2, 144), low(2, 144), low(2, 2, 144), low(2, 4, 144), low(2, 144),
            low(2, 2, 288),
            pltpu.VMEM((2, 8, features), F32),
            pltpu.VMEM((4, 8, features), F32),
            pltpu.VMEM((4, 8, features), F32),
            pltpu.VMEM((4, 8, features), F32),
            dma((12,)), dma((14,)), dma((14,)),
        ]
        + [dma((2, 6))] * 14
        + [dma((10,)), dma((10,)), dma((2,)), dma((2,)), dma((6,))],
        compiler_params=pltpu.CompilerParams(
            collective_id=5, has_side_effects=True, vmem_limit_bytes=60 * 2**20
        ),
        cost_estimate=pl.CostEstimate(
            flops=12 * 10**9, bytes_accessed=60 * 10**6, transcendentals=0
        ),
        name="sum_gradients",
    )(*operands, gain)


def doc_numbers(lengths, positions):
    doc_ends = jnp.cumsum(lengths)
    return jnp.sum((positions[:, None] >= doc_ends[None, :]).astype(jnp.int32), axis=1)


def swapped(block):
    return lax.ppermute(block, "section", [(0, 1), (1, 0)])


def body(tokens, cotangent, doc_lengths, norm_gains, w_qkv, w_out, w_up, w_down):
    batches, rows, features = tokens.shape
    share = w_qkv.shape[1]
    seq_rows = rows * lax.axis_size("tensor")
    section = lax.axis_index("section")
    is_first = section == 0

    def choose(zero_side, one_side):
        return jnp.where(is_first, zero_side, one_side)

    own_tokens = lax.dynamic_index_in_dim(tokens, section, 0, keepdims=False)
    own_cotangent = lax.dynamic_index_in_dim(cotangent, section, 0, keepdims=False)
    lengths = lax.dynamic_index_in_dim(doc_lengths, section, 0, keepdims=False)
    own_places = lax.axis_index("tensor") * rows + jnp.arange(rows, dtype=jnp.int32)
    all_places = jnp.arange(seq_rows, dtype=jnp.int32)
    own_docs = doc_numbers(lengths, own_places)
    all_docs = doc_numbers(lengths, all_places)
    allowed = (all_places[None, :] <= own_places[:, None]) & (
        all_docs[None, :] == own_docs[:, None]
    )
    bias = jnp.where(allowed, 0.0, -1e30).astype(F32)
    bias_turned = bias.T

    feed = (w_up[0], swapped(w_up[0]), w_down[0], swapped(w_down[0]))
    shard = jnp.stack(
        [w_qkv[0, :, :features], w_qkv[0, :, features : 2 * features], w_qkv[0, :, 2 * features :],
         w_out[0]]
    )
    gain_shard = jnp.pad(norm_gains[0], ((0, 14), (0, 0)))
    at_mine, at_theirs, gain_mine, gain_theirs = gather_weights(shard, gain_shard)
    attention = (
        at_mine.reshape(4, features, features), at_theirs.reshape(4, features, features)
    )

    def whole_gains(block):
        return block[:, :2].transpose(1, 0, 2).reshape(2, features).astype(F32)

    gain_mine, gain_theirs = whole_gains(gain_mine), whole_gains(gain_theirs)
    gains = (choose(gain_mine, gain_theirs), choose(gain_theirs, gain_mine))

    inputs = own_tokens
    saved = []
    for layer in range(2):
        results = forward_layer(layer, inputs, bias, gains[layer], attention, feed)
        saved.append((inputs,) + tuple(results))
        inputs = results[0]

    grad = own_cotangent
    pieces = [None, None]
    gain_grads = [None, None]
    for layer in (1, 0):
        (x, y, middle, normed_one, query, key, value, mixed, normed_two, act, hidden) = saved[layer]
        (grad, gain_grads[layer], out_all, pre_grad, branch, dquery, dkey, dvalue) = backward_layer(
            layer, x, grad, bias_turned, gains[layer], middle, query, key, value, act,
            attention, feed,
        )
        pieces[layer] = (
            normed_two, pre_grad, hidden, out_all, normed_one, mixed, dquery, dkey, dvalue, branch,
            y, grad,
        )
    operands = [member[layer] for member in zip(*pieces) for layer in range(2)]
    gain_rows = jnp.concatenate(gain_grads + [jnp.zeros((4, features), F32)], axis=0)
    feed_both, feed_other, at_both, at_other, activations, input_grads, gain_total = sum_gradients(
        features, rows, operands, gain_rows
    )
    gain_own = lax.dynamic_slice(
        gain_total, (2 * section, lax.axis_index("tensor") * share), (2, share)
    )
    feed_kept = lax.dynamic_index_in_dim(feed_both, section, 0, keepdims=False)
    at_kept = lax.dynamic_index_in_dim(at_both, section, 0, keepdims=False)

    def wide(block):
        return block.reshape(features, features).astype(F32)[None]

    first_half = choose(at_kept, at_other)[:, :share].astype(F32)
    other_half = choose(at_other, at_kept)[:, :share].astype(F32)
    grad_qkv = jnp.concatenate([first_half[0], first_half[1], other_half[0]], axis=1)
    return (
        activations[None],
        input_grads[None],
        gain_own[None],
        grad_qkv[None],
        other_half[1][None],
        wide(choose(feed_kept, feed_other)),
        wide(choose(feed_other, feed_kept)),
    )


def solution(mesh):
    placed = (
        P("dp", "tensor", None),
        P("dp", "tensor", None),
        P("dp", None),
        P("section", None, "tensor"),
        P("section", "tensor", None),
        P("section", "tensor", None),
        P("section", None, "tensor"),
        P("section", "tensor", None),
    )
    return jax.shard_map(
        body,
        mesh=mesh,
        in_specs=placed,
        out_specs=(
            P("section", "dp", "tensor", None),
            P("section", "dp", "tensor", None),
            P("section", None, "tensor"),
            P("section", "tensor", None),
            P("section", "tensor", None),
            P("section", None, "tensor"),
            P("section", "tensor", None),
        ),
        check_vma=False,
    )
```

time: 661 us -> 490 us (0.74)
  the two profiles are of different devices: /device:TPU:0 before, /device:TPU:1 now
where the time goes in v2:
time: 490 us; the launch traced here: 481 us
  Pallas kernels  446 us (91%)
  local copies, waits for them, and re-layouts  17.7 us (4%)
  other arithmetic  14.4 us (3%)
    pallas_call x1, Pallas kernels, sum_gradients(): pl.pallas_call(functools.partial(gradient_kernel, features), out_shape=(o...  191 us
    pallas_call x2, Pallas kernels, backward_layer(): pl.pallas_call(functools.partial(backward_kernel, layer, features), out_s...  90.9 us
    pallas_call x2, Pallas kernels, forward_layer(): pl.pallas_call(functools.partial(forward_kernel, layer, features), out_sh...  88.8 us
    pallas_call x1, Pallas kernels, gather_weights(): pl.pallas_call(weights_kernel, out_shape=(full, full, gains, gains), in_s...  75.3 us
  transfers between devices with their start and end apart: 2, of which 0 were waited for; matrix products, arithmetic and copies ran while one was open for 2% of the time, Pallas kernels for 16%

profile of v2, /device:TPU:1, one launch (start us, length us, event | category | flops | bytes accessed | tf_op | source)
XLA Modules:
  0.0 480.9 jit_solution(2420343895568273354)
XLA Ops:
  0.6 0.0 copy-start
  0.6 0.0 copy-start.5
  0.7 1.5 collective-permute-start
  2.2 0.1 collective-permute-start.1
  2.3 0.0 copy-done
  2.3 0.2 reduce-window.8
  2.4 1.3 pad.4.gain_ref
  3.7 1.8 fusion.8
  5.5 0.0 copy-done.5
  5.5 1.9 pad_maximum_fusion.shard_ref
  7.4 0.0 copy-start.8
  7.4 0.0 copy-start.9
  7.4 75.3 %gather_weights.1 = (bf16[4,4,272,1088]{3,2,1,0:T(8,128)(2,1)}, bf16[4,4,272,1088]{3,2,1,0:T(8,128)(2,1)}, bf16[4,16,272]{2,1,0:T(8,128)(2,1)}, bf16[4,16,272]{2,1,0:T(8,128)(2,1)}) custom-call(bf16[4,272,1088]{2,1,0:T(8,128)(2,1)} %pad_maximum_fusion.shard_ref, bf16[16,272]{1,0:T(8,128)(2,1)} %pad.4.gain_ref), custom_call_target="tpu_custom_call" | custom-call | bytes 60000000 | tf_op jit(solution)/shard_map/gather_weights/pallas_call | solution.py:675
  82.7 0.8 fusion.5
  83.5 0.7 select_n.72.gains_ref
  84.2 0.7 select_n.75.gains_ref
  84.9 0.1 pad.7.clone
  84.9 0.1 convert_reduce_fusion
  85.0 0.1 convert_reduce_fusion.1
  85.1 0.8 fusion.3.bias_ref
  85.9 0.8 fusion.1.bias_ref
  86.7 0.0 copy-done.8
  86.7 0.0 copy-done.9
  86.7 0.8 dynamic-slice_bitcast_fusion.1
  87.5 0.0 collective-permute-done.up_theirs
  87.5 0.0 copy-start.2
  87.5 0.0 collective-permute-done.1.down_theirs
  87.5 1.4 copy-done.2
  88.9 46.1 %layer_forward_0.1 = (bf16[96,1088]{1,0:T(8,128)(2,1)}, f32[96,1088]{1,0:T(8,128)}, bf16[96,1088]{1,0:T(8,128)(2,1)}, bf16[96,1088]{1,0:T(8,128)(2,1)}, bf16[4,9...) custom-call(bf16[96,1088]{1,0:T(8,128)(2,1)} %get-tuple-element.115., ...), custom_call_target="tpu_custom_call" | custom-call | flops 3000000000 | bytes 24000000 | tf_op jit(solution)/shard_map/layer_forward_0/pallas_call | solution.py:395
  135.1 42.6 %layer_forward_1.1 = (bf16[96,1088]{1,0:T(8,128)(2,1)}, f32[96,1088]{1,0:T(8,128)}, bf16[96,1088]{1,0:T(8,128)(2,1)}, bf16[96,1088]{1,0:T(8,128)(2,1)}, bf16[4,9...) custom-call(bf16[96,1088]{1,0:T(8,128)(2,1)} %get-tuple-element.59.x, ...), custom_call_target="tpu_custom_call" | custom-call | flops 3000000000 | bytes 24000000 | tf_op jit(solution)/shard_map/layer_forward_1/pallas_call | solution.py:395
  177.7 45.6 %layer_backward_1.1 = (bf16[96,1088]{1,0:T(8,128)(2,1)}, f32[2,1088]{1,0:T(2,128)}, bf16[4,96,1088]{2,1,0:T(8,128)(2,1)}, bf16[4,96,1088]{2,1,0:T(8,128)(2,1)}, ...) custom-call(bf16[96,1088]{1,0:T(8,128)(2,1)} %get-tuple-element.59.x_r, ...), custom_call_target="tpu_custom_call" | custom-call | flops 4000000000 | bytes 24000000 | tf_op jit(solution)/shard_map/layer_backward_1/pallas_call | solution.py:525
  223.3 0.0 copy-start.10
  223.3 45.3 %layer_backward_0.1 = (bf16[96,1088]{1,0:T(8,128)(2,1)}, f32[2,1088]{1,0:T(2,128)}, bf16[4,96,1088]{2,1,0:T(8,128)(2,1)}, bf16[4,96,1088]{2,1,0:T(8,128)(2,1)}, ...) custom-call(bf16[96,1088]{1,0:T(8,128)(2,1)} %get-tuple-element.115.x_, ...), custom_call_target="tpu_custom_call" | custom-call | flops 4000000000 | bytes 24000000 | tf_op jit(solution)/shard_map/layer_backward_0/pallas_call | solution.py:525
  268.6 0.0 copy-done.10
  268.6 1.4 maximum_maximum_fusion.refs_24_
  270.0 191.0 %sum_gradients.1 = (bf16[2,4,272,1088]{3,2,1,0:T(8,128)(2,1)}, bf16[4,272,1088]{2,1,0:T(8,128)(2,1)}, bf16[2,2,288,1088]{3,2,1,0:T(8,128)(2,1)}, bf16[2,288,1088...) custom-call(bf16[4,96,1088]{2,1,0:T(8,128)(2,1)} %get-tuple-element.58.refs_0_,, ...), custom_call_target="tpu_custom_call" | custom-call | flops 12000000000 | bytes 60000000 | tf_op jit(solution)/shard_map/sum_gradients/pallas_call | solution.py:1019
  461.0 2.9 bitcast_select_fusion
  463.9 2.6 bitcast_convert_fusion
  466.5 0.0 copy-start.4
  466.5 2.6 bitcast_convert_fusion.1
  469.1 0.0 copy-start.3
  469.1 0.3 copy-done.4
  469.4 0.1 dynamic-slice_bitcast_fusion
  469.5 1.0 copy-done.3
  470.5 0.3 select_convert_fusion
  470.9 1.2 fusion.7
  472.1 1.2 slice_bitcast_fusion.1
  473.3 0.0 copy-start.7
  473.3 0.0 copy-start.6
  473.3 0.0 copy-start.1
  473.3 4.2 concatenate.7
  477.4 1.4 dynamic-slice_bitcast_fusion.3
  478.8 0.0 copy-done.7
  478.8 0.8 copy.21
  479.6 0.0 copy-done.6
  479.6 0.8 copy.22
  480.4 0.0 copy-done.1
  (5 shorter events, 0.0 us)
Async XLA Ops:
  0.6 1.6 copy-start
  0.6 4.9 %copy-start.5 = (bf16[1,272,1088]{2,1,0:T(8,128)(2,1)S(1)}, bf16[1,272,1088]{2,1,0:T(8,128)(2,1)}, u32[]{:S(2)}) copy-start(bf16[1,272,1088]{2,1,0:T(8,128)(2,1)} %param.13) | copy-start | bytes 1775620
  0.7 86.8 %collective-permute-start = (bf16[1088,1088]{1,0:T(8,128)(2,1)}, bf16[1088,1088]{1,0:T(8,128)(2,1)S(1)}, u32[]{:S(2)}, u32[]{:S(2)}) collective-permute-start(bf16[1088,1088]{1,0:T(8,128)(2,1)} %bitcast.48), channel_id=1, source_target_pairs={{0,64},{64,0},{1,65},{65,1},{2,66},{66,2},{3,67},{67,3},{4,68},{68... | collective-permute-start | bytes 7102472 | tf_op jit(solution)/shard_map/ppermute | solution.py:1058
  2.2 85.3 %collective-permute-start.1 = (bf16[1088,1088]{1,0:T(8,128)(2,1)}, bf16[1088,1088]{1,0:T(8,128)(2,1)}, u32[]{:S(2)}, u32[]{:S(2)}) collective-permute-start(bf16[1088,1088]{1,0:T(8,128)(2,1)} %bitcast.53), channel_id=1, source_target_pairs={{0,64},{64,0},{1,65},{65,1},{2,66},{66,2},{3,67},{67,3},{4,68},{68... | collective-permute-start | bytes 7102472 | tf_op jit(solution)/shard_map/ppermute | solution.py:1058
  7.4 79.3 %copy-start.8 = (bf16[2,96,1088]{2,1,0:T(8,128)(2,1)S(1)}, bf16[2,96,1088]{2,1,0:T(8,128)(2,1)}, u32[]{:S(2)}) copy-start(bf16[2,96,1088]{2,1,0:T(8,128)(2,1)} %param.9) | copy-start | bytes 1253380
  7.4 79.3 %copy-start.9 = (bf16[2,96,1088]{2,1,0:T(8,128)(2,1)S(1)}, bf16[2,96,1088]{2,1,0:T(8,128)(2,1)}, u32[]{:S(2)}) copy-start(bf16[2,96,1088]{2,1,0:T(8,128)(2,1)} %param.8) | copy-start | bytes 1253380
  87.5 1.5 copy-start.2
  223.3 45.3 %copy-start.10 = (f32[2,1088]{1,0:T(2,128)S(1)}, f32[2,1088]{1,0:T(2,128)}, u32[]{:S(2)}) copy-start(f32[2,1088]{1,0:T(2,128)} %get-tuple-element.93) | copy-start | bytes 26116
  466.5 2.9 copy-start.4
  469.1 1.4 copy-start.3
  473.3 5.5 %copy-start.7 = (bf16[2,96,1088]{2,1,0:T(8,128)(2,1)S(1)}, bf16[2,96,1088]{2,1,0:T(8,128)(2,1)}, u32[]{:S(2)}) copy-start(bf16[2,96,1088]{2,1,0:T(8,128)(2,1)} %get-tuple-element.94) | copy-start | bytes 1253380
  473.3 6.3 %copy-start.6 = (bf16[2,96,1088]{2,1,0:T(8,128)(2,1)S(1)}, bf16[2,96,1088]{2,1,0:T(8,128)(2,1)}, u32[]{:S(2)}) copy-start(bf16[2,96,1088]{2,1,0:T(8,128)(2,1)} %get-tuple-element.95) | copy-start | bytes 1253380
  473.3 7.1 %copy-start.1 = (s32[2,4]{1,0:T(2,128)S(1)}, s32[2,4]{1,0:T(2,128)}, u32[]{:S(2)}) copy-start(s32[2,4]{1,0:T(2,128)} %param.10) | copy-start | bytes 100

commit v3 on v2

--- a/solution.py
+++ b/solution.py
@@ -410,14 +410,21 @@
     )(x, bias, gains, *attention, *feed)
 
 
-def backward_kernel(
-    layer, features, x_ref, dy_ref, bias_ref, gains_ref, middle_ref, query_ref, key_ref, value_ref,
-    act_ref, at_mine, at_theirs, up_mine, up_theirs, down_mine, down_theirs,
-    dx_ref, gain_ref, out_ref, pre_ref, branch_ref, dquery_ref, dkey_ref, dvalue_ref,
-    at_w, up_w, down_w, weight_sems, parts, landing, passing, arrived, parts_b, landing_b,
-    passing_b, arrived_b, parts_c, landing_c, passing_c, arrived_c, mixed_grad,
-    out_send, out_recv, sum_send, sum_recv, key_send, key_recv, value_send, value_recv,
-):
+def backward_kernel(layer, features, *refs):
+    take = iter(refs)
+
+    def some(count):
+        return [next(take) for _ in range(count)]
+
+    (x_ref, dy_ref, bias_ref, gains_ref, middle_ref, query_ref, key_ref, value_ref, act_ref,
+     at_mine, at_theirs, up_mine, up_theirs, down_mine, down_theirs) = some(15)
+    operands = some(10) if layer == 0 else None
+    (dx_ref, gain_ref, out_ref, pre_ref, branch_ref, dquery_ref, dkey_ref, dvalue_ref) = some(8)
+    results = some(4) if layer == 0 else None
+    (at_w, up_w, down_w, weight_sems, parts, landing, passing, arrived, parts_b, landing_b,
+     passing_b, arrived_b, parts_c, landing_c, passing_c, arrived_c, mixed_grad, kept_grad,
+     out_send, out_recv, sum_send, sum_recv, key_send, key_recv, value_send, value_recv) = some(26)
+    extra = GradientSum(1, features, operands, results, take) if layer == 0 else None
     ring = Ring("x")
     me = ring.me
     fetches = attention_weights(layer, at_mine, at_theirs, at_w, weight_sems)
@@ -427,9 +434,14 @@
         fetches[which][0]()
     rows = x_ref.shape[0]
     out_ref[me] = dy_ref[...]
-    greet(ring.to_right, ring.to_left)
+    if extra is None:
+        greet(ring.to_right, ring.to_left)
+    else:
+        greet_all()
     grads = row_gather(ring, out_ref, (out_send, out_recv))
     grads.start()
+    if extra is not None:
+        extra.start_inputs()
     sums = row_scatter(ring, parts, landing, passing, arrived, (sum_send, sum_recv))
     fetches[5][1]()
     fetches[4][1]()
@@ -439,8 +451,14 @@
         pre_ref[block] = (hidden_grad * gelu_slope(act_ref[block])).astype(LOW)
         parts[block] = dot_nt(pre_ref[block], up_w[...]).astype(LOW)
 
+    def steps(*names):
+        if extra is not None:
+            for name in names:
+                getattr(extra, name)()
+
     feed(me)
     grads.relay()
+    steps("feed_products")
     grads.wait_left()
     feed(ring.left)
     grads.wait_right()
@@ -449,16 +467,22 @@
     grads.wait_opposite()
     feed(ring.opposite)
     sums.start_far()
+    steps("products_0", "feed_relay")
     sums.relay()
+    steps("products_1")
     middle_part, gain_two = norm_back(middle_ref[...], gains_ref[1:2, :], row_total(sums))
     gain_ref[1:2, :] = gain_two
     middle_grad = dy_ref[...].astype(F32) + middle_part
-    middle_ref_grad = middle_grad
+    kept_grad[...] = middle_grad
     branch_ref[...] = middle_grad.astype(LOW)
     fetches[3][1]()
     mixed_grad[...] = dot_nt(branch_ref[...], at_w[3]).astype(LOW)
     bias = bias_ref[...]
-    for begin, width in pair_columns(features):
+    dkeys = row_scatter(ring, parts_b, landing_b, passing_b, arrived_b, (key_send, key_recv))
+    dvalues = row_scatter(
+        ring, parts_c, landing_c, passing_c, arrived_c, (value_send, value_recv)
+    )
+    for count, (begin, width) in enumerate(pair_columns(features)):
         columns = pl.ds(begin, width)
         queries = query_ref[:, columns]
         outer = mixed_grad[:, columns]
@@ -484,10 +508,10 @@
         dquery_ref[:, columns] = (dquery * 0.125).astype(LOW)
         parts_b[:, :, columns] = (dkey * 0.125).astype(LOW).reshape(4, rows, width)
         parts_c[:, :, columns] = dvalue.astype(LOW).reshape(4, rows, width)
-    dkeys = row_scatter(ring, parts_b, landing_b, passing_b, arrived_b, (key_send, key_recv))
-    dvalues = row_scatter(
-        ring, parts_c, landing_c, passing_c, arrived_c, (value_send, value_recv)
-    )
+        if count == 2:
+            steps("feed_middle", "x_relay_0")
+        if count == 5:
+            steps("feed_middle_relay", "x_relay_1")
     dkeys.start_far()
     dvalues.start_far()
     dkeys.start_near()
@@ -495,21 +519,35 @@
     for which in (0, 1, 2):
         fetches[which][1]()
     one_grad = dot_nt(dquery_ref[...], at_w[0])
+    steps("feed_end")
     dkeys.relay()
     dvalues.relay()
+    steps("start_0", "feed_end_relay")
     dkey_ref[...] = row_total(dkeys).astype(LOW)
+    one_grad = one_grad + dot_nt(dkey_ref[...], at_w[1])
+    steps("start_1", "relay_0")
     dvalue_ref[...] = row_total(dvalues).astype(LOW)
-    one_grad = one_grad + dot_nt(dkey_ref[...], at_w[1]) + dot_nt(dvalue_ref[...], at_w[2])
+    one_grad = one_grad + dot_nt(dvalue_ref[...], at_w[2])
     inputs_part, gain_one = norm_back(x_ref[...].astype(F32), gains_ref[0:1, :], one_grad)
     gain_ref[0:1, :] = gain_one
-    dx_ref[...] = (middle_ref_grad + inputs_part).astype(LOW)
+    dx_ref[...] = (kept_grad[...] + inputs_part).astype(LOW)
+    steps("relay_1", "middle_0", "middle_relay_0", "feed_hand", "middle_1", "end_0", "middle_relay_1",
+          "end_relay_0", "end_1", "end_relay_1", "hand", "finish")
     grads.finish()
     sums.finish()
     dkeys.finish()
     dvalues.finish()
 
 
-def backward_layer(layer, x, dy, bias, gains, middle, query, key, value, act, attention, feed):
+def greet_all():
+    rings = [Ring(axis) for axis in ("x", "y", "z")]
+    greet(
+        *[ring.to_right for ring in rings], *[ring.to_left for ring in rings], sibling()
+    )
+
+
+def backward_layer(layer, x, dy, bias, gains, middle, query, key, value, act, attention, feed,
+                   operands=()):
     rows, features = x.shape
     hidden = feed[0].shape[1]
     out_shape = (
@@ -522,26 +560,28 @@
         jax.ShapeDtypeStruct((rows, features), LOW),
         jax.ShapeDtypeStruct((rows, features), LOW),
     )
+    sums = gradient_outputs(features) if layer == 0 else ()
     return pl.pallas_call(
         functools.partial(backward_kernel, layer, features),
-        out_shape=out_shape,
-        in_specs=[in_vmem()] * 9 + [anywhere()] * 6,
-        out_specs=[in_vmem()] * len(out_shape),
+        out_shape=out_shape + sums,
+        in_specs=[in_vmem()] * 9 + [anywhere()] * (6 + len(operands)),
+        out_specs=[in_vmem()] * len(out_shape) + [anywhere()] * len(sums),
         scratch_shapes=weight_scratch(features, hidden)
         + scatter_scratch(rows, features) * 3
-        + [pltpu.VMEM((rows, features), LOW)]
-        + [pltpu.SemaphoreType.DMA((6,))] * 8,
+        + [pltpu.VMEM((rows, features), LOW), pltpu.VMEM((rows, features), F32)]
+        + [pltpu.SemaphoreType.DMA((6,))] * 8
+        + (gradient_scratch(features, rows) if layer == 0 else []),
         compiler_params=pltpu.CompilerParams(
-            collective_id=2 + layer, has_side_effects=True, vmem_limit_bytes=56 * 2**20
+            collective_id=2 + layer, has_side_effects=True, vmem_limit_bytes=62 * 2**20
         ),
         cost_estimate=pl.CostEstimate(
             flops=4 * 10**9, bytes_accessed=24 * 10**6, transcendentals=10**6
         ),
         name=f"layer_backward_{layer}",
-    )(x, dy, bias, gains, middle, query, key, value, act, *attention, *feed)
-
-
-X_ROWS, Y_ROWS = 48, 112
+    )(x, dy, bias, gains, middle, query, key, value, act, *attention, *feed, *operands)
+
+
+X_ROWS, Y_ROWS = 96, 96
 
 
 def weights_kernel(
@@ -555,8 +595,8 @@
     y_begin, z_begin = X_ROWS, X_ROWS + Y_ROWS
     z_rows = share - z_begin
     all_x, all_y, all_z = pl.ds(0, X_ROWS), pl.ds(y_begin, Y_ROWS), pl.ds(z_begin, z_rows)
-    y_half = (pl.ds(y_begin, 64), pl.ds(y_begin + 64, Y_ROWS - 64))
-    z_half = (pl.ds(z_begin, 64), pl.ds(z_begin + 64, z_rows - 64))
+    y_half = (pl.ds(y_begin, 48), pl.ds(y_begin + 48, Y_ROWS - 48))
+    z_half = (pl.ds(z_begin, 48), pl.ds(z_begin + 48, z_rows - 48))
     pair = sibling()
     greet(
         x_ring.to_right, x_ring.to_left, y_ring.to_right, y_ring.to_left, z_ring.to_right,
@@ -624,9 +664,9 @@
         copy.start()
     gain_copy(0, mine_x, gain_ref).start()
     gain_copy(1, mine_x, gain_ref).start()
-    along_x.start()
     first_y.relay()
     first_z.relay()
+    along_x.start()
     first_y.wait_all()
     locals_[0].wait()
     along_y.start()
@@ -714,62 +754,369 @@
             self.copy(which, self.ring.me).wait_send()
 
 
+class PlaneSum:
+    def __init__(self, near, far, source, out, size, first, scratch, sems, keep):
+        self.landing, self.passing, self.arrived, self.mid, self.done = scratch
+        self.out, self.size, self.near, self.far, self.keep = out, size, near, far, keep
+        self.halves = ((0, first), (first, size - first))
+
+        def rows(block, half):
+            begin, count = self.halves[half]
+            return pl.ds(pl.multiple_of(block * size + begin, 16), count)
+
+        def half_rows(half):
+            return pl.ds(*self.halves[half])
+
+        self.half_rows = half_rows
+        self.scatter = Scatter(
+            near,
+            lambda block, half: source.at[rows(block, half)],
+            lambda half: self.landing.at[half_rows(half)],
+            lambda half: self.passing.at[half_rows(half)],
+            lambda side, half: self.arrived.at[side, half_rows(half)],
+            sems[0],
+        )
+        self.gather = Gather(far, lambda block, half: self.mid.at[block, half_rows(half)], sems[1])
+        self.spread = Gather(
+            near,
+            lambda block, half: out.at[rows(block, half)],
+            sems[2],
+            lambda half: self.done.at[half_rows(half)],
+        )
+
+    def start(self):
+        self.scatter.start_far()
+        self.scatter.start_near()
+
+    def relay(self):
+        self.scatter.relay()
+
+    def middle(self):
+        self.scatter.wait()
+        for half in range(2):
+            self.mid[self.far.me, self.half_rows(half)] = self.scatter.total(half).astype(LOW)
+        self.gather.start()
+
+    def middle_relay(self):
+        self.gather.relay()
+
+    def own(self):
+        place = pl.ds(pl.multiple_of(self.near.me * self.size, 16), self.size)
+        return pltpu.make_async_copy(self.done, self.out.at[place], self.keep)
+
+    def end(self):
+        self.gather.wait_all()
+        four = [self.mid[block].astype(F32) for block in range(4)]
+        self.done[...] = ((four[0] + four[1]) + (four[2] + four[3])).astype(LOW)
+        self.spread.start()
+        self.own().start()
+
+    def end_relay(self):
+        self.spread.relay()
+
+    def wait(self):
+        self.spread.wait_all()
+        self.own().wait()
+
+    def finish(self):
+        self.scatter.finish()
+        self.gather.finish()
+        self.spread.finish()
+
+
+FEED_BLOCK, AT_BLOCK = 144, 80
+
+
+def gradient_outputs(features):
+    feed = jax.ShapeDtypeStruct((2, 4 * FEED_BLOCK, features), LOW)
+    attention = jax.ShapeDtypeStruct((2, 4 * AT_BLOCK, features), LOW)
+    return (feed, feed, attention, attention)
+
+
+def gradient_scratch(features, rows):
+    share = features // 4
+    dma = pltpu.SemaphoreType.DMA
+
+    def low(*shape):
+        return pltpu.VMEM(shape + (features,), LOW)
+
+    def plane(size):
+        return [low(size), low(size), low(2, size), low(4, size), low(size)] + [dma((6,))] * 6
+
+    return (
+        [low(2, 2, 4, rows), low(2, 2, rows), low(2, 2, rows), low(2, features),
+         low(2, 4 * FEED_BLOCK), low(2, 4 * AT_BLOCK)]
+        + ([low(share), low(share), low(2, share)] + [dma((6,))] * 2) * 2
+        + plane(FEED_BLOCK) * 2
+        + plane(AT_BLOCK) * 2
+        + [dma((6,)), dma((6,)), dma((6,)), dma((4,)), dma((2,)), dma((2,))]
+    )
+
+
+class GradientSum:
+    def __init__(self, layer, features, operands, results, take):
+        self.layer, self.features = layer, features
+        self.operands = operands
+        self.feed_out, self.feed_other, self.at_out, self.at_other = results
+        (self.feed_in, self.at_left, self.at_right, self.at_sum, self.feed_sum,
+         self.at_kept) = [next(take) for _ in range(6)]
+        self.pair, self.section = sibling(), lax.axis_index("section")
+        x_ring, y_ring, z_ring = Ring("x"), Ring("y"), Ring("z")
+        share = features // 4
+        self.share = share
+        self.across = []
+        for which in range(2):
+            landing, passing, arrived, send, recv = [next(take) for _ in range(5)]
+            halves = ((0, 144), (144, share - 144))
+
+            def part(block, half, which=which, halves=halves):
+                begin, count = halves[half]
+                row = pl.multiple_of(block * share + begin, 16)
+                return self.at_sum.at[which, pl.ds(row, count)]
+
+            def cut(ref, halves=halves):
+                return lambda half: ref.at[pl.ds(*halves[half])]
+
+            self.across.append(
+                Scatter(
+                    x_ring, part, cut(landing), cut(passing),
+                    lambda side, half, arrived=arrived, halves=halves: arrived.at[
+                        side, pl.ds(*halves[half])
+                    ],
+                    (send, recv),
+                )
+            )
+        self.halves = halves
+        planes = []
+        for which in range(4):
+            scratch = [next(take) for _ in range(5)]
+            sems = [next(take) for _ in range(6)]
+            planes.append((scratch, [tuple(sems[i : i + 2]) for i in (0, 2, 4)]))
+        (self.local_sems, swap_send, swap_recv, keep, end_send, end_recv) = [
+            next(take) for _ in range(6)
+        ]
+        self.swap, self.end_sems = (swap_send, swap_recv), (end_send, end_recv)
+        orders = ((y_ring, z_ring), (z_ring, y_ring))
+        self.feed, self.attention = [], []
+        for which in range(2):
+            self.feed.append(
+                PlaneSum(
+                    *orders[which], self.feed_sum.at[which], self.feed_out.at[which], FEED_BLOCK,
+                    80, *planes[which], keep.at[which],
+                )
+            )
+            self.attention.append(
+                PlaneSum(
+                    *orders[which], self.at_kept.at[which], self.at_out.at[which], AT_BLOCK, 48,
+                    *planes[2 + which], keep.at[2 + which],
+                )
+            )
+
+    def inputs(self, first):
+        two, pre, hidden, out, one, mixed, dq, dk, dv, branch = self.operands
+        zero = (two, pre, one, one, dq, dk)
+        other = (hidden, out, one, mixed, dv, branch)
+        own, sent = (zero, other) if first else (other, zero)
+        targets = (
+            self.feed_in.at[0], self.feed_in.at[1], self.at_left.at[0], self.at_left.at[1],
+            self.at_right.at[0], self.at_right.at[1],
+        )
+
+        def keep(which):
+            return pltpu.make_async_copy(
+                own[which], targets[which].at[0], self.local_sems.at[which]
+            )
+
+        def send(which):
+            return remote(sent[which], targets[which].at[1], self.swap, which, self.pair)
+
+        return keep, send
+
+    def start_inputs(self):
+        for first in (True, False):
+
+            @pl.when(self.section == (0 if first else 1))
+            def _(first=first):
+                keep, send = self.inputs(first)
+                for which in range(6):
+                    send(which).start()
+                for which in range(6):
+                    keep(which).start()
+
+    def wait_inputs(self, whiches):
+        keep, send = self.inputs(True)
+        for which in whiches:
+            keep(which).wait()
+            send(which).wait_recv()
+
+    def feed_products(self):
+        self.wait_inputs((0, 1))
+        features, whole = self.features, 4 * FEED_BLOCK
+        right = self.feed_in[1].reshape(-1, features)
+        for begin in range(0, features, 256):
+            count = min(256, features - begin)
+            left = self.feed_in[0, :, :, :, pl.ds(begin, count)].reshape(-1, count)
+            product = dot_tn(left, right).astype(LOW)
+            first = max(0, min(count, whole - begin))
+            if first:
+                self.feed_sum[0, pl.ds(begin, first)] = product[:first]
+            if first < count:
+                self.feed_sum[1, pl.ds(begin + first - whole, count - first)] = product[first:]
+        spare = 2 * whole - features
+        self.feed_sum[1, pl.ds(whole - spare, spare)] = jnp.zeros((spare, features), LOW)
+        for plane in self.feed:
+            plane.start()
+
+    def products(self, which):
+        self.wait_inputs((2 + which, 4 + which))
+        features = self.features
+        right = self.at_right[which].reshape(-1, features)
+        for begin in range(0, features, 256):
+            count = min(256, features - begin)
+            left = self.at_left[which, :, :, pl.ds(begin, count)].reshape(-1, count)
+            self.at_sum[which, pl.ds(begin, count)] = dot_tn(left, right).astype(LOW)
+        self.across[which].start_far()
+        self.across[which].start_near()
+
+    def products_0(self):
+        self.products(0)
+
+    def products_1(self):
+        self.products(1)
+
+    def feed_relay(self):
+        for plane in self.feed:
+            plane.relay()
+
+    def feed_middle(self):
+        for plane in self.feed:
+            plane.middle()
+
+    def feed_middle_relay(self):
+        for plane in self.feed:
+            plane.middle_relay()
+
+    def feed_end(self):
+        for plane in self.feed:
+            plane.end()
+
+    def feed_end_relay(self):
+        for plane in self.feed:
+            plane.end_relay()
+
+    def x_relay_0(self):
+        self.across[0].relay()
+
+    def x_relay_1(self):
+        self.across[1].relay()
+
+    def attention_start(self, which):
+        across = self.across[which]
+        across.wait()
+        for half in range(2):
+            self.at_kept[which, pl.ds(*self.halves[half])] = across.total(half).astype(LOW)
+        spare = 4 * AT_BLOCK - self.share
+        self.at_kept[which, pl.ds(self.share, spare)] = jnp.zeros((spare, self.features), LOW)
+        self.attention[which].start()
+
+    def start_0(self):
+        self.attention_start(0)
+
+    def start_1(self):
+        self.attention_start(1)
+
+    def relay_0(self):
+        self.attention[0].relay()
+
+    def relay_1(self):
+        self.attention[1].relay()
+
+    def middle_0(self):
+        self.attention[0].middle()
+
+    def middle_1(self):
+        self.attention[1].middle()
+
+    def middle_relay_0(self):
+        self.attention[0].middle_relay()
+
+    def middle_relay_1(self):
+        self.attention[1].middle_relay()
+
+    def end_0(self):
+        self.attention[0].end()
+
+    def end_1(self):
+        self.attention[1].end()
+
+    def end_relay_0(self):
+        self.attention[0].end_relay()
+
+    def end_relay_1(self):
+        self.attention[1].end_relay()
+
+    def ends(self, which):
+        src, dst = ((self.feed_out, self.feed_other), (self.at_out, self.at_other))[which]
+        return remote(src, dst, self.end_sems, which, self.pair)
+
+    def give(self, which):
+        @pl.when(self.section != self.layer)
+        def _():
+            self.ends(which).start()
+
+    def feed_hand(self):
+        for plane in self.feed:
+            plane.wait()
+        self.give(0)
+
+    def hand(self):
+        for plane in self.attention:
+            plane.wait()
+        self.give(1)
+
+    def finish(self):
+        _, send = self.inputs(True)
+        for which in range(6):
+            send(which).wait_send()
+        for each in self.across + self.feed + self.attention:
+            each.finish()
+
+        @pl.when(self.section != self.layer)
+        def _():
+            self.ends(0).wait_send()
+            self.ends(1).wait_send()
+
+        @pl.when(self.section == self.layer)
+        def _():
+            self.ends(0).wait_recv()
+            self.ends(1).wait_recv()
+
+
 def gradient_kernel(features, *refs):
-    (two_a, two_b, pre_a, pre_b, hid_a, hid_b, out_a, out_b, one_a, one_b, mix_a, mix_b, dq_a, dq_b,
-     dk_a, dk_b, dv_a, dv_b, br_a, br_b, y_a, y_b, dx_a, dx_b, gain_in,
-     feed_out, feed_other, at_out, at_other, act_out, grad_out, gain_out,
-     feed_in, at_left, at_right, at_sum, feed_sum,
-     xl, xp, xa, fl, fp, fa, fs, fr, al, ap, aa, as_, ar, ad, gain_pair, gain_x, gain_y, gain_z,
-     local_sems, swap_send, swap_recv, x_send, x_recv, f_send, f_recv, fg_send, fg_recv, fh_send,
-     fh_recv, a_send, a_recv, ag_send, ag_recv, ah_send, ah_recv, gain_send, gain_recv, end_send,
-     end_recv, keep_sems) = refs
+    take = iter(refs)
+
+    def some(count):
+        return [next(take) for _ in range(count)]
+
+    operands = some(10)
+    y_a, y_b, dx_a, dx_b, gain_in = some(5)
+    results = some(4)
+    act_out, grad_out, gain_out = some(3)
+    sums = GradientSum(0, features, operands, results, take)
+    (gain_pair, gain_x, gain_y, gain_z, gain_send, gain_recv, last_send, last_recv,
+     keep_sems) = some(9)
     x_ring, y_ring, z_ring = Ring("x"), Ring("y"), Ring("z")
-    pair = sibling()
-    section = lax.axis_index("section")
-    share = features // 4
-    greet(
-        x_ring.to_right, x_ring.to_left, y_ring.to_right, y_ring.to_left, z_ring.to_right,
-        z_ring.to_left, pair,
-    )
-    layers = (
-        (two_a, pre_a, hid_a, out_a, one_a, mix_a, dq_a, dk_a, dv_a, br_a, y_a, dx_a),
-        (two_b, pre_b, hid_b, out_b, one_b, mix_b, dq_b, dk_b, dv_b, br_b, y_b, dx_b),
-    )
-
-    def both(layer, first):
-        (two, pre, hidden, out, one, mixed, dq, dk, dv, branch, _, _) = layers[layer]
-        zero = (one, one, dq, dk, two, pre)
-        other = (one, mixed, dv, branch, hidden, out)
-        own, sent = (zero, other) if first else (other, zero)
-        targets = [
-            at_left.at[layer, 0], at_left.at[layer, 1], at_right.at[layer, 0],
-            at_right.at[layer, 1], feed_in.at[layer, 0], feed_in.at[layer, 1],
-        ]
-        keeps = [
-            pltpu.make_async_copy(ref, target.at[0], local_sems.at[layer * 6 + which])
-            for which, (ref, target) in enumerate(zip(own, targets))
-        ]
-        sends = [
-            remote(ref, target.at[1], (swap_send, swap_recv), layer * 6 + which, pair)
-            for which, (ref, target) in enumerate(zip(sent, targets))
-        ]
-        return keeps, sends
-
-    def start_inputs(first):
-        for which in range(6):
-            for layer in (1, 0):
-                for copy in both(layer, first):
-                    copy[which].start()
-
-    def last_copies(layer):
-        _, _, _, _, _, _, _, _, _, _, y, dx = layers[layer]
+    pair, section = sibling(), lax.axis_index("section")
+    greet_all()
+    sums.start_inputs()
+
+    def last_copies(y, dx):
         return (
-            remote(y, act_out.at[section], (swap_send, swap_recv), 12, pair),
-            remote(dx, grad_out.at[section], (swap_send, swap_recv), 13, pair),
+            remote(y, act_out.at[section], (last_send, last_recv), 0, pair),
+            remote(dx, grad_out.at[section], (last_send, last_recv), 1, pair),
         )
 
-    def keep_copies(layer):
-        _, _, _, _, _, _, _, _, _, _, y, dx = layers[layer]
+    def keep_copies(y, dx):
         return (
             pltpu.make_async_copy(y, act_out.at[section], keep_sems.at[0]),
             pltpu.make_async_copy(dx, grad_out.at[section], keep_sems.at[1]),
@@ -777,167 +1124,20 @@
 
     @pl.when(section == 0)
     def _():
-        start_inputs(True)
-        for copy in last_copies(1) + keep_copies(0):
+        for copy in last_copies(y_b, dx_b) + keep_copies(y_a, dx_a):
             copy.start()
 
     @pl.when(section == 1)
     def _():
-        start_inputs(False)
-        for copy in last_copies(0) + keep_copies(1):
+        for copy in last_copies(y_a, dx_a) + keep_copies(y_b, dx_b):
             copy.start()
 
     gain_pair[0] = gain_in[...]
     swap_gain = remote(gain_pair.at[0], gain_pair.at[1], (gain_send, gain_recv), 9, pair)
     swap_gain.start()
-
-    def wait_inputs(layer, whiches):
-        keeps, sends = both(layer, True)
-        for which in whiches:
-            keeps[which].wait()
-            sends[which].wait_recv()
-
-    x_sums, f_sums, f_mids, f_ends, a_sums, a_mids, a_ends = [], [], [], [], [], [], []
-    f_half = ((0, 144), (144, share - 144))
-    a_half = ((0, 80), (80, 64))
-    for layer in range(2):
-
-        def x_part(block, half, layer=layer):
-            return at_sum.at[layer, half, pl.ds(pl.multiple_of(block * share, 16), share)]
-
-        def pick(ref, layer=layer):
-            return lambda half: ref.at[layer, half]
-
-        def pick_side(ref, halves, layer=layer):
-            return lambda side, half: ref.at[layer, side, pl.ds(*halves[half])]
-
-        def pick_half(ref, halves, layer=layer):
-            return lambda half: ref.at[layer, pl.ds(*halves[half])]
-
-        def pick_slot(ref, halves, layer=layer):
-            return lambda block, half: ref.at[layer, block, pl.ds(*halves[half])]
-
-        def sems(send, recv, layer=layer):
-            return send.at[layer], recv.at[layer]
-
-        def f_part(block, half, layer=layer):
-            begin, size = f_half[half]
-            return feed_sum.at[layer, pl.ds(pl.multiple_of(block * share + begin, 16), size)]
-
-        def a_part(block, half, layer=layer):
-            begin, size = a_half[half]
-            row = lax.rem(block, 2) * 144 + begin
-            return ad.at[layer, lax.div(block, 2), pl.ds(pl.multiple_of(row, 16), size)]
-
-        def a_out(block, half, layer=layer):
-            begin, size = a_half[half]
-            row = lax.rem(block, 2) * 144 + begin
-            return at_out.at[layer, lax.div(block, 2), pl.ds(pl.multiple_of(row, 16), size)]
-
-        x_sums.append(
-            Scatter(
-                x_ring, x_part, pick(xl), pick(xp),
-                lambda side, half, layer=layer: xa.at[layer, side, half], sems(x_send, x_recv),
-            )
-        )
-        near, far = (y_ring, z_ring) if layer == 0 else (z_ring, y_ring)
-        f_sums.append(
-            Scatter(
-                near, f_part, pick_half(fl, f_half), pick_half(fp, f_half),
-                pick_side(fa, f_half), sems(f_send, f_recv),
-            )
-        )
-        f_mids.append(Gather(far, pick_slot(fs, f_half), sems(fg_send, fg_recv)))
-        f_ends.append(
-            Gather(near, pick_slot(feed_out, f_half), sems(fh_send, fh_recv), pick_half(fr, f_half))
-        )
-        a_sums.append(
-            Scatter(
-                near, a_part, pick_half(al, a_half), pick_half(ap, a_half),
-                pick_side(aa, a_half), sems(a_send, a_recv),
-            )
-        )
-        a_mids.append(Gather(far, pick_slot(as_, a_half), sems(ag_send, ag_recv)))
-        a_ends.append(Gather(near, a_out, sems(ah_send, ah_recv), pick_half(ar, a_half)))
-
-    chunks = [(begin, min(256, features - begin)) for begin in range(0, features, 256)]
-
-    def attention_products(layer):
-        wait_inputs(layer, (0, 1, 2, 3))
-        for which in range(2):
-            right = at_right[layer, which].reshape(-1, features)
-            for begin, size in chunks:
-                left = at_left[layer, which, :, :, pl.ds(begin, size)].reshape(-1, size)
-                at_sum[layer, which, pl.ds(begin, size)] = dot_tn(left, right).astype(LOW)
-        x_sums[layer].start_far()
-        x_sums[layer].start_near()
-
-    def feed_products(layer):
-        wait_inputs(layer, (4, 5))
-        right = feed_in[layer, 1].reshape(-1, features)
-        for begin, size in chunks:
-            left = feed_in[layer, 0, :, :, :, pl.ds(begin, size)].reshape(-1, size)
-            feed_sum[layer, pl.ds(begin, size)] = dot_tn(left, right).astype(LOW)
-        f_sums[layer].start_far()
-        f_sums[layer].start_near()
-
-    def feed_middle(layer):
-        f_sums[layer].wait()
-        place = f_mids[layer].ring.me
-        for half in range(2):
-            fs[layer, place, pl.ds(*f_half[half])] = f_sums[layer].total(half).astype(LOW)
-        f_mids[layer].start()
-
-    def four(ref, layer, halves, half):
-        rows = pl.ds(*halves[half])
-        return (ref[layer, 0, rows].astype(F32) + ref[layer, 1, rows].astype(F32)) + (
-            ref[layer, 2, rows].astype(F32) + ref[layer, 3, rows].astype(F32)
-        )
-
-    def feed_end(layer):
-        f_mids[layer].wait_all()
-        for half in range(2):
-            fr[layer, pl.ds(*f_half[half])] = four(fs, layer, f_half, half).astype(LOW)
-        f_ends[layer].start()
-        pltpu.make_async_copy(
-            fr.at[layer], feed_out.at[layer, f_ends[layer].ring.me], keep_sems.at[2 + layer]
-        ).start()
-
-    def attention_middle(layer):
-        x_sums[layer].wait()
-        for half in range(2):
-            ad[layer, half, pl.ds(0, share)] = x_sums[layer].total(half).astype(LOW)
-            ad[layer, half, pl.ds(share, 288 - share)] = jnp.zeros((288 - share, features), LOW)
-        a_sums[layer].start_far()
-        a_sums[layer].start_near()
-
-    def attention_far(layer):
-        a_sums[layer].wait()
-        place = a_mids[layer].ring.me
-        for half in range(2):
-            as_[layer, place, pl.ds(*a_half[half])] = a_sums[layer].total(half).astype(LOW)
-        a_mids[layer].start()
-
-    def own_attention(layer):
-        block = a_ends[layer].ring.me
-        row = pl.multiple_of(lax.rem(block, 2) * 144, 16)
-        return pltpu.make_async_copy(
-            ar.at[layer], at_out.at[layer, lax.div(block, 2), pl.ds(row, 144)],
-            keep_sems.at[4 + layer],
-        )
-
-    def attention_end(layer):
-        a_mids[layer].wait_all()
-        for half in range(2):
-            ar[layer, pl.ds(*a_half[half])] = four(as_, layer, a_half, half).astype(LOW)
-        a_ends[layer].start()
-        own_attention(layer).start()
-
-    attention_products(1)
-    attention_products(0)
-    feed_products(0)
-    feed_products(1)
-
+    sums.products_0()
+    sums.products_1()
+    sums.feed_products()
     swap_gain.wait()
     gain_x[x_ring.me] = gain_pair[0] + gain_pair[1]
     small = [
@@ -945,108 +1145,67 @@
         for i, (ring, slots) in enumerate(((x_ring, gain_x), (y_ring, gain_y), (z_ring, gain_z)))
     ]
     small[0].start()
-    x_sums[1].relay()
-    f_sums[0].relay()
-    f_sums[1].relay()
+    sums.x_relay_0()
+    sums.x_relay_1()
+    sums.feed_relay()
     small[0].relay()
-    feed_middle(0)
-    feed_middle(1)
+    sums.start_0()
+    sums.feed_middle()
     gain_y[y_ring.me] = small[0].result()
     small[1].start()
-    f_mids[0].relay()
-    f_mids[1].relay()
-    x_sums[0].relay()
+    sums.relay_0()
+    sums.feed_middle_relay()
     small[1].relay()
-    attention_middle(1)
-    feed_end(0)
-    feed_end(1)
+    sums.start_1()
+    sums.middle_0()
+    sums.feed_end()
     gain_z[z_ring.me] = small[1].result()
     small[2].start()
-    a_sums[1].relay()
-    f_ends[0].relay()
-    f_ends[1].relay()
+    sums.relay_1()
+    sums.middle_relay_0()
+    sums.feed_end_relay()
     small[2].relay()
-    attention_far(1)
-    attention_middle(0)
-    a_mids[1].relay()
-    attention_end(1)
-    a_sums[0].relay()
-    a_ends[1].relay()
+    sums.middle_1()
+    sums.end_0()
+    sums.middle_relay_1()
     gain_out[...] = small[2].result()
-
-    for layer in range(2):
-        f_ends[layer].wait_all()
-        pltpu.make_async_copy(
-            fr.at[layer], feed_out.at[layer, f_ends[layer].ring.me], keep_sems.at[2 + layer]
-        ).wait()
-    end_feed = remote(feed_out.at[1 - section], feed_other, (end_send, end_recv), 0, pair)
-    end_feed.start()
-
-    attention_far(0)
-    a_mids[0].relay()
-    attention_end(0)
-    a_ends[0].relay()
-    for layer in (1, 0):
-        a_ends[layer].wait_all()
-        own_attention(layer).wait()
-    end_attention = remote(at_out.at[1 - section], at_other, (end_send, end_recv), 1, pair)
-    end_attention.start()
-    for layer in range(2):
-        for copy in both(layer, True)[1]:
-            copy.wait_send()
-        for many in (x_sums, f_sums, f_mids, f_ends, a_sums, a_mids, a_ends):
-            many[layer].finish()
+    sums.end_relay_0()
+    sums.end_1()
+    sums.feed_hand()
+    sums.end_relay_1()
+    sums.hand()
+    sums.finish()
     for each in small:
         each.finish()
-    for copy in last_copies(0):
+    for copy in last_copies(y_a, dx_a) + keep_copies(y_a, dx_a):
         copy.wait()
-    for copy in keep_copies(0):
-        copy.wait()
-    end_feed.wait()
-    end_attention.wait()
-
-
-def sum_gradients(features, rows, operands, gain):
-    share = features // 4
+
+
+def sum_gradients(features, rows, operands, last, gain):
     dma = pltpu.SemaphoreType.DMA
-
-    def low(*shape):
-        return pltpu.VMEM(shape + (features,), LOW)
-
-    def out(*shape):
-        return jax.ShapeDtypeStruct(shape + (features,), LOW)
-
+    small = [pltpu.VMEM((4, 8, features), F32)] * 3
     return pl.pallas_call(
         functools.partial(gradient_kernel, features),
-        out_shape=(
-            out(2, 4, share), out(4, share), out(2, 2, 288), out(2, 288), out(2, rows),
-            out(2, rows), jax.ShapeDtypeStruct((8, features), F32),
+        out_shape=gradient_outputs(features)
+        + (
+            jax.ShapeDtypeStruct((2, rows, features), LOW),
+            jax.ShapeDtypeStruct((2, rows, features), LOW),
+            jax.ShapeDtypeStruct((8, features), F32),
         ),
-        in_specs=[anywhere()] * 24 + [in_vmem()],
+        in_specs=[anywhere()] * 14 + [in_vmem()],
         out_specs=[anywhere()] * 6 + [in_vmem()],
-        scratch_shapes=[
-            low(2, 2, 2, 4, rows), low(2, 2, 2, rows), low(2, 2, 2, rows),
-            low(2, 2, features), low(2, features),
-            low(2, 2, share), low(2, 2, share), low(2, 2, 2, share),
-            low(2, share), low(2, share), low(2, 2, share), low(2, 4, share), low(2, share),
-            low(2, 144), low(2, 144), low(2, 2, 144), low(2, 4, 144), low(2, 144),
-            low(2, 2, 288),
-            pltpu.VMEM((2, 8, features), F32),
-            pltpu.VMEM((4, 8, features), F32),
-            pltpu.VMEM((4, 8, features), F32),
-            pltpu.VMEM((4, 8, features), F32),
-            dma((12,)), dma((14,)), dma((14,)),
-        ]
-        + [dma((2, 6))] * 14
-        + [dma((10,)), dma((10,)), dma((2,)), dma((2,)), dma((6,))],
+        scratch_shapes=gradient_scratch(features, rows)
+        + [pltpu.VMEM((2, 8, features), F32)]
+        + small
+        + [dma((10,)), dma((10,)), dma((2,)), dma((2,)), dma((2,))],
         compiler_params=pltpu.CompilerParams(
             collective_id=5, has_side_effects=True, vmem_limit_bytes=60 * 2**20
         ),
         cost_estimate=pl.CostEstimate(
-            flops=12 * 10**9, bytes_accessed=60 * 10**6, transcendentals=0
+            flops=6 * 10**9, bytes_accessed=60 * 10**6, transcendentals=0
         ),
         name="sum_gradients",
-    )(*operands, gain)
+    )(*operands, *last, gain)
 
 
 def doc_numbers(lengths, positions):
@@ -1106,34 +1265,32 @@
         inputs = results[0]
 
     grad = own_cotangent
-    pieces = [None, None]
-    gain_grads = [None, None]
+    gain_grads, input_grads, operands = [None, None], [None, None], ()
     for layer in (1, 0):
-        (x, y, middle, normed_one, query, key, value, mixed, normed_two, act, hidden) = saved[layer]
-        (grad, gain_grads[layer], out_all, pre_grad, branch, dquery, dkey, dvalue) = backward_layer(
+        (x, _, middle, normed_one, query, key, value, mixed, normed_two, act, hidden) = saved[layer]
+        results = backward_layer(
             layer, x, grad, bias_turned, gains[layer], middle, query, key, value, act,
-            attention, feed,
+            attention, feed, operands,
         )
-        pieces[layer] = (
+        (grad, gain_grads[layer], out_all, pre_grad, branch, dquery, dkey, dvalue) = results[:8]
+        input_grads[layer] = grad
+        operands = (
             normed_two, pre_grad, hidden, out_all, normed_one, mixed, dquery, dkey, dvalue, branch,
-            y, grad,
         )
-    operands = [member[layer] for member in zip(*pieces) for layer in range(2)]
+    sums_one = results[8:]
     gain_rows = jnp.concatenate(gain_grads + [jnp.zeros((4, features), F32)], axis=0)
-    feed_both, feed_other, at_both, at_other, activations, input_grads, gain_total = sum_gradients(
-        features, rows, operands, gain_rows
+    *sums_zero, activations, input_grads, gain_total = sum_gradients(
+        features, rows, operands, (saved[0][1], saved[1][1], *input_grads), gain_rows
     )
     gain_own = lax.dynamic_slice(
         gain_total, (2 * section, lax.axis_index("tensor") * share), (2, share)
     )
-    feed_kept = lax.dynamic_index_in_dim(feed_both, section, 0, keepdims=False)
-    at_kept = lax.dynamic_index_in_dim(at_both, section, 0, keepdims=False)
-
-    def wide(block):
-        return block.reshape(features, features).astype(F32)[None]
-
-    first_half = choose(at_kept, at_other)[:, :share].astype(F32)
-    other_half = choose(at_other, at_kept)[:, :share].astype(F32)
+
+    def whole(block):
+        return block.reshape(-1, features)[:features].astype(F32)[None]
+
+    first_half = choose(sums_zero[2], sums_one[3])[:, :share].astype(F32)
+    other_half = choose(sums_zero[3], sums_one[2])[:, :share].astype(F32)
     grad_qkv = jnp.concatenate([first_half[0], first_half[1], other_half[0]], axis=1)
     return (
         activations[None],
@@ -1141,8 +1298,8 @@
         gain_own[None],
         grad_qkv[None],
         other_half[1][None],
-        wide(choose(feed_kept, feed_other)),
-        wide(choose(feed_other, feed_kept)),
+        whole(choose(sums_zero[0], sums_one[1])),
+        whole(choose(sums_zero[1], sums_one[0])),
     )
 
 

time: 490 us -> 476 us (0.971)
  the two profiles are of different devices: /device:TPU:1 before, /device:TPU:0 now
where the time goes in v3:
time: 476 us; the launch traced here: 467 us
  Pallas kernels  433 us (91%)
  local copies, waits for them, and re-layouts  17.9 us (4%)
  other arithmetic  14.4 us (3%)
    pallas_call x2, Pallas kernels, backward_layer(): pl.pallas_call(functools.partial(backward_kernel, layer, features), out_s...  168 us
    pallas_call x1, Pallas kernels, sum_gradients(): pl.pallas_call(functools.partial(gradient_kernel, features), out_shape=gr...  104 us
    pallas_call x2, Pallas kernels, forward_layer(): pl.pallas_call(functools.partial(forward_kernel, layer, features), out_sh...  96.6 us
    pallas_call x1, Pallas kernels, gather_weights(): pl.pallas_call(weights_kernel, out_shape=(full, full, gains, gains), in_s...  64.3 us
  transfers between devices with their start and end apart: 2, of which 0 were waited for; matrix products, arithmetic and copies ran while one was open for 2% of the time, Pallas kernels for 14%

profile of v3, /device:TPU:0, one launch (start us, length us, event | category | flops | bytes accessed | tf_op | source)
XLA Modules:
  0.0 466.5 jit_solution(4650725281934087428)
XLA Ops:
  0.6 0.0 copy-start
  0.6 0.0 copy-start.9
  0.7 0.1 collective-permute-start
  0.8 0.5 collective-permute-start.1
  1.2 0.1 copy-done
  1.3 0.2 reduce-window.8
  1.5 1.3 pad.4.gain_ref
  2.8 1.8 fusion.12
  4.6 0.0 copy-done.9
  4.6 1.9 pad_maximum_fusion.shard_ref
  6.5 0.0 copy-start.12
  6.5 0.0 copy-start.13
  6.5 64.3 %gather_weights.1 = (bf16[4,4,272,1088]{3,2,1,0:T(8,128)(2,1)}, bf16[4,4,272,1088]{3,2,1,0:T(8,128)(2,1)}, bf16[4,16,272]{2,1,0:T(8,128)(2,1)}, bf16[4,16,272]{2,1,0:T(8,128)(2,1)}) custom-call(bf16[4,272,1088]{2,1,0:T(8,128)(2,1)} %pad_maximum_fusion.shard_ref, bf16[16,272]{1,0:T(8,128)(2,1)} %pad.4.gain_ref), custom_call_target="tpu_custom_call" | custom-call | bytes 60000000 | tf_op jit(solution)/shard_map/gather_weights/pallas_call | solution.py:715
  70.8 0.8 fusion.9
  71.6 0.7 select_n.68.gains_ref.refs_3_
  72.2 0.7 select_n.72.gains_ref.refs_3_
  72.9 0.1 pad.7.clone
  73.0 0.1 convert_reduce_fusion
  73.1 0.1 convert_reduce_fusion.1
  73.2 0.8 fusion.7.bias_ref
  73.9 0.8 fusion.5.refs_2_
  74.7 0.0 copy-done.12
  74.7 0.0 copy-done.13
  74.7 0.8 dynamic-slice_bitcast_fusion
  75.5 0.0 collective-permute-done.up_theirs.refs_12_
  75.5 0.0 collective-permute-done.1.down_theirs.refs_14_
  75.5 50.4 %layer_forward_0.1 = (bf16[96,1088]{1,0:T(8,128)(2,1)}, f32[96,1088]{1,0:T(8,128)}, bf16[96,1088]{1,0:T(8,128)(2,1)}, bf16[96,1088]{1,0:T(8,128)(2,1)}, bf16[4,9...) custom-call(bf16[96,1088]{1,0:T(8,128)(2,1)} %get-tuple-element.119., ...), custom_call_target="tpu_custom_call" | custom-call | flops 3000000000 | bytes 24000000 | tf_op jit(solution)/shard_map/layer_forward_0/pallas_call | solution.py:395
  125.9 46.2 %layer_forward_1.1 = (bf16[96,1088]{1,0:T(8,128)(2,1)}, f32[96,1088]{1,0:T(8,128)}, bf16[96,1088]{1,0:T(8,128)(2,1)}, bf16[96,1088]{1,0:T(8,128)(2,1)}, bf16[4,9...) custom-call(bf16[96,1088]{1,0:T(8,128)(2,1)} %get-tuple-element.63.x, ...), custom_call_target="tpu_custom_call" | custom-call | flops 3000000000 | bytes 24000000 | tf_op jit(solution)/shard_map/layer_forward_1/pallas_call | solution.py:395
  172.1 47.6 %layer_backward_1.1 = (bf16[96,1088]{1,0:T(8,128)(2,1)}, f32[2,1088]{1,0:T(2,128)}, bf16[4,96,1088]{2,1,0:T(8,128)(2,1)}, bf16[4,96,1088]{2,1,0:T(8,128)(2,1)}, ...) custom-call(bf16[96,1088]{1,0:T(8,128)(2,1)} %get-tuple-element.63.x_r, ...), custom_call_target="tpu_custom_call" | custom-call | flops 4000000000 | bytes 24000000 | tf_op jit(solution)/shard_map/layer_backward_1/pallas_call | solution.py:564
  219.7 0.0 copy-start.14
  219.7 120.7 %layer_backward_0.1 = (bf16[96,1088]{1,0:T(8,128)(2,1)}, f32[2,1088]{1,0:T(2,128)}, bf16[4,96,1088]{2,1,0:T(8,128)(2,1)}, bf16[4,96,1088]{2,1,0:T(8,128)(2,1)}, ...) custom-call(bf16[96,1088]{1,0:T(8,128)(2,1)} %get-tuple-element.119., ...), custom_call_target="tpu_custom_call" | custom-call | flops 4000000000 | bytes 24000000 | tf_op jit(solution)/shard_map/layer_backward_0/pallas_call | solution.py:564
  340.4 0.0 copy-done.14
  340.4 1.4 maximum_maximum_fusion.refs_14_
  341.8 0.0 copy-start.3
  341.8 103.6 %sum_gradients.1 = (bf16[2,576,1088]{2,1,0:T(8,128)(2,1)}, bf16[2,576,1088]{2,1,0:T(8,128)(2,1)}, bf16[2,320,1088]{2,1,0:T(8,128)(2,1)}, bf16[2,320,1088]{2,1,0:...) custom-call(bf16[4,96,1088]{2,1,0:T(8,128)(2,1)} %get-tuple-element.62.refs_0_, ...), custom_call_target="tpu_custom_call" | custom-call | flops 6000000000 | bytes 60000000 | tf_op jit(solution)/shard_map/sum_gradients/pallas_call | solution.py:1187
  445.4 0.0 copy-done.3
  445.4 2.3 broadcast_select_fusion
  447.7 0.0 copy-start.2
  447.7 0.0 copy-start.4
  447.7 2.9 fusion
  450.6 0.0 copy-done.2
  450.6 1.5 copy-done.4
  452.0 0.3 broadcast_select_fusion.1
  452.3 0.0 copy-start.6
  452.3 0.0 copy-start.8
  452.3 2.6 fusion.1
  455.0 0.0 copy-done.6
  455.0 0.5 copy-done.8
  455.5 0.2 fusion.2
  455.6 0.0 copy-start.5
  455.6 0.0 copy-start.7
  455.6 1.2 fusion.11
  456.8 0.6 copy-done.5
  457.5 0.4 copy-done.7
  457.9 0.2 fusion.3
  458.1 1.2 slice_bitcast_fusion.3
  459.3 0.0 copy-start.11
  459.3 4.2 concatenate.7
  463.5 1.4 dynamic-slice_bitcast_fusion.2
  464.8 0.0 copy-done.11
  464.8 0.8 copy.21
  465.6 0.0 copy-done.10
  465.6 0.8 copy.22
  466.4 0.0 copy-done.1
  (7 shorter events, 0.0 us)
Async XLA Ops:
  0.6 0.7 copy-start
  0.6 3.9 copy-start.9
  0.7 74.9 %collective-permute-start = (bf16[1088,1088]{1,0:T(8,128)(2,1)}, bf16[1088,1088]{1,0:T(8,128)(2,1)}, u32[]{:S(2)}, u32[]{:S(2)}) collective-permute-start(bf16[1088,1088]{1,0:T(8,128)(2,1)} %bitcast.47), channel_id=1, source_target_pairs={{0,64},{64,0},{1,65},{65,1},{2,66},{66,2},{3,67},{67,3},{4,68},{68... | collective-permute-start | bytes 7102472 | tf_op jit(solution)/shard_map/ppermute | solution.py:1217
  0.8 74.8 %collective-permute-start.1 = (bf16[1088,1088]{1,0:T(8,128)(2,1)}, bf16[1088,1088]{1,0:T(8,128)(2,1)}, u32[]{:S(2)}, u32[]{:S(2)}) collective-permute-start(bf16[1088,1088]{1,0:T(8,128)(2,1)} %bitcast.52), channel_id=1, source_target_pairs={{0,64},{64,0},{1,65},{65,1},{2,66},{66,2},{3,67},{67,3},{4,68},{68... | collective-permute-start | bytes 7102472 | tf_op jit(solution)/shard_map/ppermute | solution.py:1217
  6.5 68.3 %copy-start.12 = (bf16[2,96,1088]{2,1,0:T(8,128)(2,1)S(1)}, bf16[2,96,1088]{2,1,0:T(8,128)(2,1)}, u32[]{:S(2)}) copy-start(bf16[2,96,1088]{2,1,0:T(8,128)(2,1)} %param.9) | copy-start | bytes 1253380
  6.5 68.3 %copy-start.13 = (bf16[2,96,1088]{2,1,0:T(8,128)(2,1)S(1)}, bf16[2,96,1088]{2,1,0:T(8,128)(2,1)}, u32[]{:S(2)}) copy-start(bf16[2,96,1088]{2,1,0:T(8,128)(2,1)} %param.8) | copy-start | bytes 1253380
  219.7 120.7 %copy-start.14 = (f32[2,1088]{1,0:T(2,128)S(1)}, f32[2,1088]{1,0:T(2,128)}, u32[]{:S(2)}) copy-start(f32[2,1088]{1,0:T(2,128)} %get-tuple-element.97) | copy-start | bytes 26116
  341.8 103.6 %copy-start.3 = (bf16[2,576,1088]{2,1,0:T(8,128)(2,1)S(1)}, bf16[2,576,1088]{2,1,0:T(8,128)(2,1)}, u32[]{:S(2)}) copy-start(bf16[2,576,1088]{2,1,0:T(8,128)(2,1)} %get-tuple-element.108) | copy-start | bytes 7520260
  447.7 2.9 copy-start.2
  447.7 4.4 copy-start.4
  452.3 2.7 copy-start.6
  452.3 3.1 copy-start.8
  455.6 1.8 copy-start.5
  455.6 2.3 copy-start.7
  459.3 5.5 %copy-start.11 = (bf16[2,96,1088]{2,1,0:T(8,128)(2,1)S(1)}, bf16[2,96,1088]{2,1,0:T(8,128)(2,1)}, u32[]{:S(2)}) copy-start(bf16[2,96,1088]{2,1,0:T(8,128)(2,1)} %get-tuple-element.98) | copy-start | bytes 1253380
  459.3 6.3 %copy-start.10 = (bf16[2,96,1088]{2,1,0:T(8,128)(2,1)S(1)}, bf16[2,96,1088]{2,1,0:T(8,128)(2,1)}, u32[]{:S(2)}) copy-start(bf16[2,96,1088]{2,1,0:T(8,128)(2,1)} %get-tuple-element.99) | copy-start | bytes 1253380
  459.3 7.1 %copy-start.1 = (s32[2,4]{1,0:T(2,128)S(1)}, s32[2,4]{1,0:T(2,128)}, u32[]{:S(2)}) copy-start(s32[2,4]{1,0:T(2,128)} %param.10) | copy-start | bytes 100
